TPU v7x, 32 devices: a whole 2x2x4 slice. The times are simulated.
32 devices in a mesh: groups: 2 (over x), store: 8 (over z, y), head: 2 (over core).
Axes of the slice: x: 2, y: 2, z: 4, core: 2. Of those that a mesh axis runs over, the one named last changes fastest.
Arguments:
- tokens_in: bfloat16 [16384, 2048], P(('groups', 'store', 'head')), parts along dimension 0, may hold values from -6 to 6
- w_query: bfloat16 [2048, 1024], P(None, 'head'), may hold values from -0.125 to 0.125
- w_key: bfloat16 [2048, 1024], P(None, 'head'), may hold values from -0.125 to 0.125
- w_value: bfloat16 [2048, 2048], P(None, 'head'), may hold values from -0.125 to 0.125
- w_zgate: bfloat16 [2048, 2048], P(None, 'head'), may hold values from -0.125 to 0.125
- w_gates: bfloat16 [2, 2048, 16], P(None, None, 'head'), may hold values from -0.125 to 0.125
- w_out: bfloat16 [2048, 2048], P('head'), may hold values from -0.125 to 0.125
- decay_log: float32 [16], P('head'), may hold values from -8.5 to -2.5
- dt_bias: float32 [16], P('head'), may hold values from -2 to 2
- norm_gain: float32 [128], replicated, may hold values from 0.1 to 1.9
- init_state: float32 [16, 128, 128], P('head'), may hold values from -8 to 8
- doc_trans: bfloat16 [64, 16, 128, 128], P(('groups', 'store'), 'head'), parts along dimension 0, may hold values from -0.15 to 1
- doc_state: bfloat16 [64, 16, 128, 128], P(('groups', 'store'), 'head'), parts along dimension 0, may hold values from -1.1953125 to 1.1953125
- retrieval: int32 [16, 16], P('groups'), parts along dimension 0, may hold values from 0 to 31, as said below
- doc_place: int32 [64], P('groups'), parts along dimension 0, may hold values from 0 to 31, as said below
- assignment: int32 [16], P('groups'), parts along dimension 0, may hold values from 0 to 7, each once
Outputs:
- layer_out: bfloat16 [16384, 2048], P(('groups', 'store', 'head')), parts along dimension 0
There are 2 independent parts, one for each index of `groups`. A program takes and returns all parts, laid end to end along the dimension named above; an argument that names none is the same for every part. Nothing has to cross between parts.
Inputs may be any that keep to these rules, and one draw needn't show every extreme that they name: `retrieval`: each row names 16 different documents; in every row at most 2 of them have doc_place in the 4 rows of one store device (equal doc_place // 4), and exactly 2 for at least one device. A permutation: document d lies in row doc_place[d] of doc_trans and doc_state.
All inputs are finite; a program needn't handle non-finite values.
Results may differ from a plain program's by a relative error of at most 0.011.
Values may be sent and summed in bfloat16 or wider, within the bound.
A program may use at most 192 MiB of HBM per device.

v0:
```python
import jax
import jax.numpy as jnp
from jax import lax
from jax.sharding import PartitionSpec as P

DK = 128
DV = 128
SPAN = 64
LIST = 16
CAP = 2


highest = lax.Precision.HIGHEST


def contract(form, left, right):
    return jnp.einsum(form, left, right, precision=highest)


def unit_lower_inverse(strict_part):
    on_diagonal = jnp.eye(strict_part.shape[-1], dtype=strict_part.dtype)
    powered = -strict_part
    inverse = on_diagonal + powered
    for doubling in range(strict_part.shape[-1].bit_length() - 2):
        powered = contract("...ij,...jk->...ik", powered, powered)
        inverse = inverse + contract("...ij,...jk->...ik", inverse, powered)
    return inverse


def normalize_rows(values, factor):
    return values * lax.rsqrt(jnp.sum(values * values, axis=-1, keepdims=True) + 1e-06) * factor


def span_terms(queries, keys_all, values, beta_rows, logdecay):
    positions = jnp.arange(SPAN)
    strict = positions[:, None] > positions[None, :]
    lower_mask = positions[:, None] >= positions[None, :]
    cumulative = jnp.cumsum(logdecay, axis=-1)
    spread = cumulative[..., :, None] - cumulative[..., None, :]
    pair_decay = jnp.exp(jnp.where(lower_mask, spread, 0.0))
    key_key = jnp.einsum("hncd,hnmd->hncm", keys_all, keys_all, preferred_element_type=jnp.float32)
    query_key = jnp.einsum("hncd,hnmd->hncm", queries, keys_all, preferred_element_type=jnp.float32)
    lower_mix = jnp.where(strict, pair_decay * key_key * beta_rows[..., None, :], 0.0)
    attend = jnp.where(lower_mask, pair_decay * query_key * beta_rows[..., None, :], 0.0)
    growth = jnp.exp(cumulative)
    inverse = unit_lower_inverse(lower_mix)
    keys_wide = keys_all.astype(jnp.float32)
    corrected = contract("hncm,hnmv->hncv", inverse, values.astype(jnp.float32))
    weighted = contract("hncm,hnmd->hncd", inverse, growth[..., None] * keys_wide)
    tail_weight = jnp.exp(cumulative[..., -1:] - cumulative) * beta_rows
    return (
        growth[..., None] * queries.astype(jnp.float32),
        attend,
        corrected,
        weighted,
        tail_weight[..., None] * keys_wide,
        growth[..., -1],
    )


def span_step(carried, block_terms):
    scaled_query, attend, corrected, weighted, tail_keys, closing = block_terms
    correction = corrected - contract("hcd,hdv->hcv", weighted, carried)
    output = contract("hcd,hdv->hcv", scaled_query, carried) + contract(
        "hcm,hmv->hcv", attend, correction
    )
    carried = closing[:, None, None] * carried + contract("hcd,hcv->hdv", tail_keys, correction)
    return (carried, output)


def prepare(proj_query, proj_key, proj_value, pre_decay, pre_beta, decay_log, dt_bias):
    tokens = proj_query.shape[0]
    heads_v = decay_log.shape[0]
    heads_k = proj_query.shape[1] // DK
    group_size = heads_v // heads_k
    queries = normalize_rows(
        proj_query.astype(jnp.float32).reshape(tokens, heads_k, DK), DK ** (-0.5)
    ).astype(jnp.bfloat16)
    keys_all = normalize_rows(
        proj_key.astype(jnp.float32).reshape(tokens, heads_k, DK), 1.0
    ).astype(jnp.bfloat16)
    queries = jnp.repeat(queries, group_size, axis=1)
    keys_all = jnp.repeat(keys_all, group_size, axis=1)
    values = proj_value.reshape(tokens, heads_v, DV)
    beta_rows = jax.nn.sigmoid(pre_beta.astype(jnp.float32))
    logdecay = -jnp.exp(decay_log) * jax.nn.softplus(pre_decay.astype(jnp.float32) + dt_bias)
    blocks = tokens // SPAN

    def heads_first(tensor):
        swapped = jnp.moveaxis(tensor, 1, 0)
        return swapped.reshape((heads_v, blocks, SPAN) + swapped.shape[2:])

    return span_terms(
        heads_first(queries),
        heads_first(keys_all),
        heads_first(values),
        heads_first(beta_rows),
        heads_first(logdecay),
    )


def compose(init_state, fetched_trans, fetched_state):

    def advance(carried, doc_pair):
        updated = contract("hij,hjv->hiv", doc_pair[0].astype(jnp.float32), carried) + doc_pair[
            1
        ].astype(jnp.float32)
        return (updated, None)

    return lax.scan(advance, init_state, (fetched_trans, fetched_state))[0]


def gated_mix(outputs, proj_gate, norm_gain):
    blocks, heads_v, block_len, feature_width = outputs.shape
    core_out = jnp.moveaxis(outputs, 1, 0).reshape(heads_v, blocks * block_len, feature_width)
    core_out = jnp.moveaxis(core_out, 0, 1)
    gate_values = proj_gate.astype(jnp.float32).reshape(core_out.shape)
    normed = (
        core_out
        * lax.rsqrt(jnp.mean(core_out * core_out, axis=-1, keepdims=True) + 1e-06)
        * norm_gain
        * jax.nn.silu(gate_values)
    )
    return normed.reshape(core_out.shape[0], heads_v * feature_width).astype(jnp.bfloat16)


def on_device(
    tokens_in,
    w_query,
    w_key,
    w_value,
    w_zgate,
    w_gates,
    w_out,
    decay_log,
    dt_bias,
    norm_gain,
    init_state,
    doc_trans,
    doc_state,
    retrieval,
    doc_place,
    assignment,
):
    heads_v = decay_log.shape[0]
    heads_k = w_query.shape[1] // DK
    width_key = heads_k * DK
    width_value = heads_v * DV
    store_count = lax.axis_size("store")
    store_rank = lax.axis_index("store")
    request = jnp.sum(
        jnp.where(jnp.arange(assignment.shape[0], dtype=jnp.int32) == store_rank, assignment, 0)
    )
    wanted_ids = jnp.sum(
        jnp.where(
            (jnp.arange(retrieval.shape[0], dtype=jnp.int32) == request)[:, None], retrieval, 0
        ),
        axis=0,
    )
    store_rows = jnp.sum(
        jnp.where(
            wanted_ids[:, None] == jnp.arange(doc_place.shape[0], dtype=jnp.int32)[None, :],
            doc_place[None, :],
            0,
        ),
        axis=1,
    )
    token_piece = lax.all_gather(tokens_in, "head", axis=0, tiled=True)
    products = [
        jnp.dot(token_piece, weight, preferred_element_type=jnp.float32)
        for weight in (w_query, w_key, w_value, w_zgate, w_gates[0], w_gates[1])
    ]
    projected = jnp.concatenate(products, axis=1).astype(jnp.bfloat16)
    proj_query = projected[:, :width_key]
    proj_key = projected[:, width_key : 2 * width_key]
    proj_value = projected[:, 2 * width_key : 2 * width_key + width_value]
    proj_gate = projected[:, 2 * width_key + width_value : 2 * width_key + 2 * width_value]
    pre_decay = projected[
        :, 2 * width_key + 2 * width_value : 2 * width_key + 2 * width_value + heads_v
    ]
    pre_beta = projected[:, 2 * width_key + 2 * width_value + heads_v :]
    owners = store_rows // doc_trans.shape[0]
    local_rows = store_rows % doc_trans.shape[0]
    earlier = jnp.arange(LIST)[:, None] > jnp.arange(LIST)[None, :]
    copy_rank = jnp.sum(
        jnp.where(earlier & (owners[:, None] == owners[None, :]), 1, 0), axis=1
    ).astype(jnp.int32)
    slot_ids = jnp.arange(store_count * CAP, dtype=jnp.int32)
    slot_owner = slot_ids // CAP
    slot_copy = slot_ids % CAP
    matches = (slot_owner[:, None] == owners[None, :]) & (slot_copy[:, None] == copy_rank[None, :])
    wanted = jnp.sum(jnp.where(matches, local_rows[None, :], 0), axis=1)
    requested = lax.all_to_all(wanted, "store", split_axis=0, concat_axis=0, tiled=True)
    replies = (
        lax.all_to_all(
            jnp.take(doc_trans, requested, axis=0), "store", split_axis=0, concat_axis=0, tiled=True
        ),
        lax.all_to_all(
            jnp.take(doc_state, requested, axis=0), "store", split_axis=0, concat_axis=0, tiled=True
        ),
    )
    positions = owners * CAP + copy_rank
    fetched_trans = jnp.take(replies[0], positions, axis=0)
    fetched_state = jnp.take(replies[1], positions, axis=0)
    block_terms = prepare(proj_query, proj_key, proj_value, pre_decay, pre_beta, decay_log, dt_bias)
    by_block = tuple((jnp.moveaxis(tensor, 1, 0) for tensor in block_terms))
    start_state = compose(init_state, fetched_trans, fetched_state)
    outputs = lax.scan(span_step, start_state, by_block)[1]
    mixed_rows = gated_mix(outputs, proj_gate, norm_gain)
    return lax.psum_scatter(
        jnp.dot(mixed_rows, w_out, preferred_element_type=jnp.float32),
        "head",
        scatter_dimension=0,
        tiled=True,
    ).astype(jnp.bfloat16)


def solution(mesh):
    in_specs = (
        P(("groups", "store", "head"), None),
        P(None, "head"),
        P(None, "head"),
        P(None, "head"),
        P(None, "head"),
        P(None, None, "head"),
        P("head", None),
        P("head"),
        P("head"),
        P(),
        P("head", None, None),
        P(("groups", "store"), "head", None, None),
        P(("groups", "store"), "head", None, None),
        P("groups", None),
        P("groups"),
        P("groups"),
    )
    out_specs = P(("groups", "store", "head"), None)
    return jax.shard_map(
        on_device, mesh=mesh, in_specs=in_specs, out_specs=out_specs, check_vma=False
    )
```

profile of v0, /device:TPU:0, one launch (start us, length us, event | category | flops | bytes accessed | tf_op | source)
XLA Modules:
  0.0 437.5 jit_solution(2654559109878916254)
XLA Ops:
  11.9 7.3 %all-to-all-start = ((s32[8,2,1]{1,2,0:T(1,128)}), s32[8,2,1]{1,2,0:T(1,128)S(1)}, u32[]{:S(2)}, u32[]{:S(2)}) async-start(s32[8,2,1]{1,2,0:T(1,128)} %bitcast.9), calls=%async_computation | async-start | bytes 8192 | tf_op jit(solution)/shard_map/all_to_all | solution.py:193
  19.2 6.4 %all-to-all-done = s32[8,2,1]{1,2,0:T(1,128)S(1)} async-done(((s32[8,2,1]{1,2,0:T(1,128)}), s32[8,2,1]{1,2,0:T(1,128)S(1)}, u32[]{:S(2)}, u32[]{:S(2)}) %all-to-all-start) | async-done | bytes 96 | tf_op jit(solution)/shard_map/all_to_all | solution.py:193
  26.9 3.0 gather_fusion
  29.9 4.4 gather_fusion.2
  34.2 7.6 %broadcast_select_fusion.2 = (bf16[16,8,128,128]{3,2,1,0:T(8,128)(2,1)}, bf16[16,8,128,128]{3,2,1,0:T(8,128)(2,1)}) fusion(bf16[16,8,128,128]{3,2,1,0:T(8,128)(2,1)} %gather_fusion.2, pred[16]{0:T(512)(128)(4,1)S(1)} %compare_and_fusion.1, bf16[16,8,128,128]{3,2,1,0:T(8,128)(2,1)} %gather_fusion), kind=kLoop, calls=%fused_computation.45 | loop fusion | flops 4194304 | bytes 16777232 | tf_op jit(solution)/shard_map/jit(_take)/select_n | solution.py:199
  41.8 4.9 %all-to-all-start.1 = ((bf16[16,8,128,128]{3,2,1,0:T(8,128)(2,1)}), bf16[16,8,128,128]{3,2,1,0:T(8,128)(2,1)}, u32[]{:S(2)}, u32[]{:S(2)}) async-start(bf16[16,8,128,128]{3,2,1,0:T(8,128)(2,1)} %get-tuple-element.156), calls=%async_computation.1 | async-start | bytes 8388608 | tf_op jit(solution)/shard_map/all_to_all | solution.py:195
  46.8 4.6 %fusion.35 = (f32[1024,4]{0,1:T(4,128)S(1)}, bf16[1024,512]{0,1:T(8,128)(2,1)S(1)}) fusion(bf16[1024,2048]{1,0:T(8,128)(2,1)} %all-gather.2.cloned.1.call-done, bf16[2048,512]{1,0:T(8,128)(2,1)S(1)} %copy-done), kind=kOutput, calls=%fused_computation.61 | convolution fusion | flops 2149576704 | bytes 7356416 | tf_op jit(solution)/shard_map/dot_general | solution.py:170
  53.0 3.4 fusion.63
  56.5 3.4 fusion.59
  60.0 8.0 %convolution_convert_fusion.1 = bf16[1024,1024]{0,1:T(8,128)(2,1)S(1)} fusion(bf16[1024,2048]{1,0:T(8,128)(2,1)} %all-gather.2.cloned.1.call-done, bf16[2048,1024]{1,0:T(8,128)(2,1)} %param.27), kind=kOutput, calls=%fused_computation.81 | convolution fusion | flops 4296015872 | bytes 10485760 | tf_op jit(solution)/shard_map/dot_general | solution.py:170
  68.0 2.6 copy.72
  70.6 5.3 %fusion.37 = (f32[1024,4]{0,1:T(4,128)S(1)}, bf16[1024,512]{0,1:T(8,128)(2,1)S(1)}) fusion(bf16[1024,2048]{1,0:T(8,128)(2,1)} %all-gather.2.cloned.1.call-done, bf16[2048,512]{1,0:T(8,128)(2,1)} %param.25), kind=kOutput, calls=%fused_computation.63 | convolution fusion | flops 2149576704 | bytes 7356416 | tf_op jit(solution)/shard_map/dot_general | solution.py:170
  79.1 8.0 %convolution_convert_fusion = bf16[1024,1024]{0,1:T(8,128)(2,1)S(1)} fusion(bf16[1024,2048]{1,0:T(8,128)(2,1)} %all-gather.2.cloned.1.call-done, bf16[2048,1024]{1,0:T(8,128)(2,1)} %param.28), kind=kOutput, calls=%fused_computation.80 | convolution fusion | flops 4296015872 | bytes 10485760 | tf_op jit(solution)/shard_map/dot_general | solution.py:170
  87.2 2.8 copy.82
  94.7 8.8 %fusion.33 = f32[8,16,64,64]{3,2,1,0:T(8,128)} fusion(f32[8,16,64,64]{3,2,1,0:T(8,128)S(1)} %fusion.75, f32[8,16,64]{2,1,0:T(8,128)S(1)} %mul.135, f32[8,16,64]{2,1,0:T(8,128)S(1)} %reduce_window_sum.11, pred[64,64]{1,0:T(8,128)(4,1)S(1)} %get-tuple-element.166, pred[64,64]{1,0:T(8,128)(4,1)S(1)} %get-tuple-element.167), kind=kOutput, calls=%fused_computation.58 | convolution fusion | flops 405798912 | bytes 4268032 | tf_op jit(solution)/shard_map/...ij,...jk->...ik/dot_general | solution.py:17
  103.5 35.2 %all-to-all-done.1 = bf16[16,8,128,128]{3,2,1,0:T(8,128)(2,1)} async-done(((bf16[16,8,128,128]{3,2,1,0:T(8,128)(2,1)}), bf16[16,8,128,128]{3,2,1,0:T(8,128)(2,1)}, u32[]{:S(2)}, u32[]{:S(2)}) %all-to-all-start.1) | async-done | bytes 4194336 | tf_op jit(solution)/shard_map/all_to_all | solution.py:195
  138.7 4.6 %all-to-all-start.2 = ((bf16[16,8,128,128]{3,2,1,0:T(8,128)(2,1)}), bf16[16,8,128,128]{3,2,1,0:T(8,128)(2,1)}, u32[]{:S(2)}, u32[]{:S(2)}) async-start(bf16[16,8,128,128]{3,2,1,0:T(8,128)(2,1)} %get-tuple-element.155), calls=%async_computation.2 | async-start | bytes 8388608 | tf_op jit(solution)/shard_map/all_to_all | solution.py:198
  143.3 8.1 %fusion.76 = f32[8,16,64,64]{3,2,1,0:T(8,128)S(1)} fusion(f32[8,16,64,64]{3,2,1,0:T(8,128)} %fusion.33), kind=kOutput, calls=%fused_computation.141 | convolution fusion | flops 402653184 | bytes 4194304 | tf_op jit(solution)/shard_map/...ij,...jk->...ik/dot_general | solution.py:17
  151.5 5.3 %fusion.78 = f32[8,16,64,64]{3,2,1,0:T(8,128)S(1)} fusion(f32[8,16,64,64]{3,2,1,0:T(8,128)S(1)} %fusion.76), kind=kOutput, calls=%fused_computation.143 | convolution fusion | flops 402653184 | bytes 4194304 | tf_op jit(solution)/shard_map/...ij,...jk->...ik/dot_general | solution.py:17
  156.8 8.1 %add_add_fusion = f32[8,16,64,64]{3,2,1,0:T(8,128)S(1)} fusion(f32[8,16,64,64]{3,2,1,0:T(8,128)S(1)} %copy-done.3, f32[8,16,64,64]{3,2,1,0:T(8,128)S(1)} %copy-done.9, f32[8,16,64]{2,1,0:T(8,128)S(1)} %mul.135, f32[8,16,64]{2,1,0:T(8,128)S(1)} %reduce_window_sum.11, f32[64,64]{1,0:T(8,128)S(1)} %fusion.70, pred[64,64]{1,0:T(8,128)(4,1)S(1)} %get-tuple-element.166, ...), kind=kOutput, calls=%fused_computation.47 | convolution fusion | flops 410517504 | bytes 6381568 | tf_op jit(solution)/shard_map/...ij,...jk->...ik/dot_general | solution.py:17
  164.9 5.8 %fusion.77 = f32[8,16,64,64]{3,2,1,0:T(8,128)} fusion(f32[8,16,64,64]{3,2,1,0:T(8,128)S(1)} %add_add_fusion, f32[8,16,64,64]{3,2,1,0:T(8,128)S(1)} %fusion.76), kind=kOutput, calls=%fused_computation.142 | convolution fusion | flops 402653184 | bytes 6291456 | tf_op jit(solution)/shard_map/...ij,...jk->...ik/dot_general | solution.py:17
  170.7 5.3 %fusion.79 = f32[8,16,64,64]{3,2,1,0:T(8,128)S(1)} fusion(f32[8,16,64,64]{3,2,1,0:T(8,128)S(1)} %fusion.78), kind=kOutput, calls=%fused_computation.144 | convolution fusion | flops 402653184 | bytes 4194304 | tf_op jit(solution)/shard_map/...ij,...jk->...ik/dot_general | solution.py:17
  176.1 6.1 %fusion.81 = f32[8,16,64,64]{3,2,1,0:T(8,128)} fusion(f32[8,16,64,64]{3,2,1,0:T(8,128)S(1)} %fusion.79), kind=kOutput, calls=%fused_computation.146 | convolution fusion | flops 402653184 | bytes 4194304 | tf_op jit(solution)/shard_map/...ij,...jk->...ik/dot_general | solution.py:17
  182.2 8.1 %convolution_add_fusion.4 = f32[8,16,64,64]{3,2,1,0:T(8,128)S(1)} fusion(f32[8,16,64,64]{3,2,1,0:T(8,128)S(1)} %fusion.78, f32[8,16,64,64]{3,2,1,0:T(8,128)S(1)} %add_add_fusion, f32[8,16,64,64]{3,2,1,0:T(8,128)} %fusion.77), kind=kOutput, calls=%fused_computation.52 | convolution fusion | flops 403701760 | bytes 8388608 | tf_op jit(solution)/shard_map/...ij,...jk->...ik/dot_general | solution.py:17
  190.3 6.3 %fusion.80 = f32[8,16,64,64]{3,2,1,0:T(8,128)} fusion(f32[8,16,64,64]{3,2,1,0:T(8,128)S(1)} %convolution_add_fusion.4, f32[8,16,64,64]{3,2,1,0:T(8,128)S(1)} %fusion.79), kind=kOutput, calls=%fused_computation.145 | convolution fusion | flops 402653184 | bytes 6291456 | tf_op jit(solution)/shard_map/...ij,...jk->...ik/dot_general | solution.py:17
  196.6 8.2 %convolution_add_fusion.3 = f32[8,16,64,64]{3,2,1,0:T(8,128)S(1)} fusion(f32[8,16,64,64]{3,2,1,0:T(8,128)S(1)} %copy-done.5, f32[8,16,64,64]{3,2,1,0:T(8,128)S(1)} %convolution_add_fusion.4, f32[8,16,64,64]{3,2,1,0:T(8,128)} %fusion.80), kind=kOutput, calls=%fused_computation.50 | convolution fusion | flops 403701760 | bytes 8388608 | tf_op jit(solution)/shard_map/...ij,...jk->...ik/dot_general | solution.py:17
  204.8 3.7 convolution_bitcast_fusion
  208.5 5.9 %fusion.34 = f32[16,8,64,128]{3,2,0,1:T(8,128)} fusion(f32[8,16,64,64]{3,2,1,0:T(8,128)S(1)} %convolution_add_fusion.3, bf16[8,16,64,128]{3,2,1,0:T(8,128)(2,1)S(1)} %bitcast.177, f32[8,16,64]{2,1,0:T(8,128)S(1)} %get-tuple-element.152), kind=kOutput, calls=%fused_computation.59 | convolution fusion | flops 807403520 | bytes 8421376 | tf_op jit(solution)/shard_map/hncm,hnmd->hncd/dot_general | solution.py:17
  214.7 3.3 fusion.26
  218.0 4.7 %fusion.19 = (f32[16,8,64,128]{3,2,0,1:T(8,128)}, f32[16,8,64,128]{3,2,0,1:T(8,128)}) fusion(bf16[8,16,64,128]{3,2,1,0:T(8,128)(2,1)S(1)} %bitcast.179, f32[8,16,64]{2,1,0:T(8,128)S(1)} %get-tuple-element.151, bf16[8,16,64,128]{3,2,1,0:T(8,128)(2,1)S(1)} %bitcast.182, f32[8,16,64]{2,1,0:T(8,128)S(1)} %get-tuple-element.152), kind=kLoop, calls=%fused_computation.30 | loop fusion | flops 4194304 | bytes 12648448 | tf_op jit(solution)/shard_map/transpose | solution.py:206
  222.7 5.2 %gather_fusion.1 = bf16[16,8,128,128]{3,2,1,0:T(8,128)(2,1)} fusion(bf16[16,8,128,128]{3,2,1,0:T(8,128)(2,1)} %all-to-all-done.1, s32[1024]{0:T(1024)S(1)} %pad_clamp_fusion), kind=kCustom, calls=%fused_computation.1.clone | custom fusion | bytes 8388672 | tf_op jit(solution)/shard_map/jit(_take)/gather | solution.py:203
  227.9 7.9 %all-to-all-done.2 = bf16[16,8,128,128]{3,2,1,0:T(8,128)(2,1)} async-done(((bf16[16,8,128,128]{3,2,1,0:T(8,128)(2,1)}), bf16[16,8,128,128]{3,2,1,0:T(8,128)(2,1)}, u32[]{:S(2)}, u32[]{:S(2)}) %all-to-all-start.2) | async-done | bytes 4194336 | tf_op jit(solution)/shard_map/all_to_all | solution.py:198
  235.8 5.2 %gather_fusion.3 = bf16[16,8,128,128]{3,2,1,0:T(8,128)(2,1)} fusion(bf16[16,8,128,128]{3,2,1,0:T(8,128)(2,1)} %all-to-all-done.2, s32[1024]{0:T(1024)S(1)} %pad_clamp_fusion), kind=kCustom, calls=%fused_computation.3.clone | custom fusion | bytes 8388672 | tf_op jit(solution)/shard_map/jit(_take)/gather | solution.py:204
  241.0 7.5 %broadcast_select_fusion = (bf16[16,8,128,128]{3,2,1,0:T(8,128)(2,1)}, bf16[16,8,128,128]{3,2,1,0:T(8,128)(2,1)}) fusion(bf16[16,8,128,128]{3,2,1,0:T(8,128)(2,1)} %gather_fusion.3, pred[16]{0:T(512)(128)(4,1)S(1)} %get-tuple-element.149, bf16[16,8,128,128]{3,2,1,0:T(8,128)(2,1)} %gather_fusion.1), kind=kLoop, calls=%fused_computation.43 | loop fusion | flops 4194304 | bytes 16777232 | tf_op jit(solution)/shard_map/jit(_take)/select_n | solution.py:204
  248.6 24.1 %while.22 = (s32[]{:T(128)}, f32[8,128,128]{2,1,0:T(8,128)S(1)}, bf16[16,8,128,128]{3,2,1,0:T(8,128)(2,1)}, bf16[16,8,128,128]{3,2,1,0:T(8,128)(2,1)}, s32[]{:T(128)}) while((s32[]{:T(128)}, f32[8,128,128]{2,1,0:T(8,128)S(1)}, bf16[16,8,128,128]{3,2,1,0:T(8,128)(2,1)}, bf16[16,8,128,128]{3,2,1,0:T(8,128)(2,1)}, s32[]{:T(128)}) %tuple.58), condition=%wide.region_6.9_spmd, body=%wide.region_5.8_spmd.sunk | while | flops 201588736 | bytes 2622525 | solution.py:110
  272.7 117.3 %while.23 = (s32[]{:T(128)}, f32[8,128,128]{2,1,0:T(8,128)S(1)}, f32[16,8,64,128]{3,2,0,1:T(8,128)}, f32[16,8]{1,0:T(8,128)S(1)}, f32[16,8,64,128]{3,2,0,1:T(8,1...) while((s32[]{:T(128)}, f32[8,128,128]{2,1,0:T(8,128)S(1)}, ...), condition=%wide.region_11.14_spmd, body=%wide.region_10.13_spmd.sunk | while | flops 352714752 | bytes 4984009 | solution.py:208
  278.0 2.1 convolution_add_fusion.8
  283.2 2.1 fusion.147
  285.3 2.1 convolution_add_fusion.8
  292.6 2.1 convolution_add_fusion.8
  297.9 2.1 fusion.147
  300.0 2.1 convolution_add_fusion.8
  307.3 2.1 convolution_add_fusion.8
  314.6 2.1 convolution_add_fusion.8
  321.9 2.1 convolution_add_fusion.8
  327.2 2.1 fusion.147
  334.5 2.1 fusion.147
  336.6 2.1 convolution_add_fusion.8
  341.9 2.1 fusion.147
  343.9 2.1 convolution_add_fusion.8
  349.2 2.1 fusion.147
  351.3 2.1 convolution_add_fusion.8
  356.5 2.1 fusion.147
  365.9 2.1 convolution_add_fusion.8
  371.2 2.1 fusion.147
  373.3 2.1 convolution_add_fusion.8
  378.5 2.1 fusion.147
  387.9 2.1 convolution_add_fusion.8
  390.0 3.5 fusion.21
  393.6 3.8 fusion.24
  397.4 2.6 copy.83
  400.0 10.6 %fusion.82 = f32[1024,2048]{1,0:T(8,128)} fusion(bf16[1024,1024]{0,1:T(8,128)(2,1)} %bitcast.184, bf16[1024,2048]{1,0:T(8,128)(2,1)} %param.30), kind=kOutput, calls=%fused_computation.147 | convolution fusion | flops 4294967296 | bytes 14680064 | tf_op jit(solution)/shard_map/dot_general | solution.py:211
  410.6 16.0 %reduce-scatter.2.cloned.1.call-done = f32[512,2048]{1,0:T(8,128)} async-done(((f32[1024,2048]{1,0:T(8,128)}), f32[512,2048]{1,0:T(8,128)}) %reduce-scatter.2.cloned.1.call-update) | async-done | bytes 4194320 | tf_op jit(solution)/shard_map/reduce_scatter | solution.py:210
  426.6 3.8 convert_element_type.55
  (161 shorter events, 111.9 us)
Async XLA Ops:
  6.5 40.3 %copy-start = (bf16[2048,512]{1,0:T(8,128)(2,1)S(1)}, bf16[2048,512]{1,0:T(8,128)(2,1)}, u32[]{:S(2)}) copy-start(bf16[2048,512]{1,0:T(8,128)(2,1)} %param.26) | copy-start | bytes 6291460
  6.5 20.3 %copy-start.6 = (bf16[4,8,128,128]{3,2,1,0:T(8,128)(2,1)S(1)}, bf16[4,8,128,128]{3,2,1,0:T(8,128)(2,1)}, u32[]{:S(2)}) copy-start(bf16[4,8,128,128]{3,2,1,0:T(8,128)(2,1)} %param.35) | copy-start | bytes 3145732
  6.5 40.3 %all-gather.2.cloned.1.call-start = ((), (), s32[]{:S(2)}) async-start(), calls=%async_computation.4 | async-start | bytes 6291456 | tf_op jit(solution)/shard_map/all_gather | solution.py:168
  11.9 13.7 %all-to-all-start = ((s32[8,2,1]{1,2,0:T(1,128)}), s32[8,2,1]{1,2,0:T(1,128)S(1)}, u32[]{:S(2)}, u32[]{:S(2)}) async-start(s32[8,2,1]{1,2,0:T(1,128)} %bitcast.9), calls=%async_computation | async-start | bytes 8192 | tf_op jit(solution)/shard_map/all_to_all | solution.py:193
  41.8 5.0 %copy-start.13 = (f32[8]{0:T(128)S(1)}, f32[8]{0:T(128)}, u32[]{:S(2)}) copy-start(f32[8]{0:T(128)} %param.31) | copy-start | bytes 100
  41.8 96.9 %all-to-all-start.1 = ((bf16[16,8,128,128]{3,2,1,0:T(8,128)(2,1)}), bf16[16,8,128,128]{3,2,1,0:T(8,128)(2,1)}, u32[]{:S(2)}, u32[]{:S(2)}) async-start(bf16[16,8,128,128]{3,2,1,0:T(8,128)(2,1)} %get-tuple-element.156), calls=%async_computation.1 | async-start | bytes 8388608 | tf_op jit(solution)/shard_map/all_to_all | solution.py:195
  51.4 1.6 copy-start.10
  51.4 1.6 copy-start.11
  92.7 2.0 copy-start.8
  138.7 97.1 %all-to-all-start.2 = ((bf16[16,8,128,128]{3,2,1,0:T(8,128)(2,1)}), bf16[16,8,128,128]{3,2,1,0:T(8,128)(2,1)}, u32[]{:S(2)}, u32[]{:S(2)}) async-start(bf16[16,8,128,128]{3,2,1,0:T(8,128)(2,1)} %get-tuple-element.155), calls=%async_computation.2 | async-start | bytes 8388608 | tf_op jit(solution)/shard_map/all_to_all | solution.py:198
  143.3 283.4 %reduce-scatter.2.cloned.1.call-start = ((), (), s32[]{:S(2)}) async-start(), calls=%async_computation.5 | async-start | bytes 12582912 | tf_op jit(solution)/shard_map/reduce_scatter | solution.py:210
  151.4 5.3 %copy-start.3 = (f32[8,16,64,64]{3,2,1,0:T(8,128)S(1)}, f32[8,16,64,64]{3,2,1,0:T(8,128)}, u32[]{:S(2)}) copy-start(f32[8,16,64,64]{3,2,1,0:T(8,128)} %fusion.33) | copy-start | bytes 6291460
  151.5 5.3 %copy-start.9 = (f32[8,16,64,64]{3,2,1,0:T(8,128)S(1)}, f32[8,16,64,64]{3,2,1,0:T(8,128)}, u32[]{:S(2)}) copy-start(f32[8,16,64,64]{3,2,1,0:T(8,128)} %copy-done.8) | copy-start | bytes 6291460
  190.2 6.3 %copy-start.5 = (f32[8,16,64,64]{3,2,1,0:T(8,128)S(1)}, f32[8,16,64,64]{3,2,1,0:T(8,128)}, u32[]{:S(2)}) copy-start(f32[8,16,64,64]{3,2,1,0:T(8,128)} %fusion.81) | copy-start | bytes 6291460
  196.6 8.2 %copy-start.7 = (bf16[8,1024,128]{2,1,0:T(8,128)(2,1)S(1)}, bf16[8,1024,128]{2,1,0:T(8,128)(2,1)}, u32[]{:S(2)}) copy-start(bf16[8,1024,128]{2,1,0:T(8,128)(2,1)} %copy.72) | copy-start | bytes 6291460
  241.0 7.5 %copy-start.2 = (f32[8,128,128]{2,1,0:T(8,128)S(1)}, f32[8,128,128]{2,1,0:T(8,128)}, u32[]{:S(2)}) copy-start(f32[8,128,128]{2,1,0:T(8,128)} %param.34) | copy-start | bytes 1572868
  390.0 3.5 copy-start.4
  390.0 3.5 copy-start.12
  410.6 19.8 %copy-start.1 = (bf16[2048,512]{1,0:T(8,128)(2,1)S(1)}, bf16[2048,512]{1,0:T(8,128)(2,1)}, u32[]{:S(2)}) copy-start(bf16[2048,512]{1,0:T(8,128)(2,1)} %param.26) | copy-start | bytes 6291460
Sparse Core Ops, SparseCore 0:
  8.9 16.3 all-gather.1
  410.7 15.8 reduce-scatter.1
where the time goes:
time: 443 us; the launch traced here: 437 us
  matrix products  267 us (60%)
  waiting for transfers between devices  66.2 us (15%)
  other arithmetic  38 us (9%)
  local copies, waits for them, and re-layouts  34.1 us (8%)
  starting transfers between devices  16.8 us (4%)
  between operations  14.1 us (3%)
    dot_general x92, matrix products, contract(): return jnp.einsum(form, left, right, precision=highest)  219 us
    all_to_all x1, waiting for transfers between devices, on_device(): lax.all_to_all(jnp.take(doc_trans, requested, axis=0), 'store', split_axi...  35.2 us
    dot_general x6, matrix products, on_device(): jnp.dot(token_piece, weight, preferred_element_type=jnp.float32)  32.7 us
    reduce_scatter x1, waiting for transfers between devices, on_device(): lax.psum_scatter(jnp.dot(mixed_rows, w_out, preferred_element_type=jnp.fl...  16 us
    dot_general x1, matrix products, on_device(): jnp.dot(mixed_rows, w_out, preferred_element_type=jnp.float32)  10.6 us
  transfers between devices with their start and end apart: 5, of which 4 were waited for; matrix products, arithmetic and copies ran while one was open for 36% of the time, Pallas kernels for 0%

commit v1 on v0

v1 whole, which is shorter than its diff:
```python
import jax
import jax.numpy as jnp
from jax import lax
from jax.experimental import pallas as pl
from jax.experimental.pallas import tpu as pltpu
from jax.sharding import PartitionSpec as P

DK = 128
DV = 128
CHUNK = 128
ROWS = 256
BF = jnp.bfloat16
F32 = jnp.float32


def mm(left, right):
    return jnp.dot(left, right, preferred_element_type=F32)


def unit_lower_inverses(mixes):
    size = mixes[0].shape[0]
    row = lax.broadcasted_iota(jnp.int32, (size, size), 0)
    col = lax.broadcasted_iota(jnp.int32, (size, size), 1)
    eye = jnp.where(row == col, 1.0, 0.0)
    inside = row // 16 == col // 16
    powers = [jnp.where(inside, -mix, 0.0) for mix in mixes]
    inverses = [eye + power for power in powers]
    powers = [mm(power.astype(BF), power.astype(BF)) for power in powers]
    for last in (False, False, True):
        if last:
            products = [mm(x.astype(BF), p.astype(BF)) for x, p in zip(inverses, powers)]
            inverses = [x + y for x, y in zip(inverses, products)]
        else:
            products = [
                mm(jnp.concatenate([x.astype(BF), p.astype(BF)], axis=0), p.astype(BF))
                for x, p in zip(inverses, powers)
            ]
            inverses = [x + y[:size] for x, y in zip(inverses, products)]
            powers = [y[size:] for y in products]
    width = 16
    while width < size:
        between = (row // (2 * width) == col // (2 * width)) & (row // width != col // width)
        narrow = [x.astype(BF) for x in inverses]
        steps = [mm(jnp.where(between, mix, 0.0).astype(BF), x) for mix, x in zip(mixes, narrow)]
        steps = [mm(x, step.astype(BF)) for x, step in zip(narrow, steps)]
        inverses = [x - step for x, step in zip(inverses, steps)]
        width *= 2
    return inverses


def delta_kernel(
    closing, x, w_q, w_k, w_v, w_z, cols, rows, gate, core, linear, q_s, k_s, v_s, qw_s, at_s, u_s, state
):
    step = pl.program_id(0)
    steps = pl.num_programs(0)
    tokens = x.shape[0]
    chunks = tokens // CHUNK
    heads = core.shape[1] // DV

    @pl.loop(0, tokens // ROWS)
    def project(tile):
        at = pl.ds(pl.multiple_of(tile * ROWS, ROWS), ROWS)
        part = x[at, :]
        q = mm(part, w_q[...]).astype(BF).astype(F32)
        q_s[at, :] = (
            q * lax.rsqrt(jnp.sum(q * q, axis=-1, keepdims=True) + 1e-06) * DK ** (-0.5)
        ).astype(BF)
        k = mm(part, w_k[...]).astype(BF).astype(F32)
        k_s[at, :] = (k * lax.rsqrt(jnp.sum(k * k, axis=-1, keepdims=True) + 1e-06)).astype(BF)
        v_s[at, :] = mm(part, w_v[...]).astype(BF)
        gate[at, :] = mm(part, w_z[...]).astype(BF)

    group = min(4, chunks)

    @pl.loop(0, chunks // group)
    def terms(quarter):
        row = lax.broadcasted_iota(jnp.int32, (CHUNK, CHUNK), 0)
        col = lax.broadcasted_iota(jnp.int32, (CHUNK, CHUNK), 1)
        kept, mixes = [], []
        for inner in range(group):
            chunk = quarter * group + inner
            at = pl.ds(pl.multiple_of(chunk * CHUNK, CHUNK), CHUNK)
            q, k, v = q_s[at, :], k_s[at, :], v_s[at, :]
            both = lax.dot_general(
                jnp.concatenate([k, q], axis=0), k, (((1,), (1,)), ((), ())), preferred_element_type=F32
            )
            k_wide = k.astype(F32)
            k_turned = k_wide.T
            for e in range(2):
                cum_c = cols[0, at, e : e + 1]
                cum_r = rows[0, e : e + 1, at]
                beta_r = rows[0, 2 + e : 3 + e, at]
                decay = jnp.exp(jnp.where(row >= col, cum_c - cum_r, 0.0)) * beta_r
                mixes.append(jnp.where(row > col, decay * both[:CHUNK], 0.0))
                attend = jnp.where(row >= col, decay * both[CHUNK:], 0.0)
                growth = jnp.exp(cum_c)
                tail = jnp.exp(cum_r[:, CHUNK - 1 :] - cum_r) * beta_r
                head = 2 * step + e
                at_s[head, chunk] = jnp.concatenate([attend, k_turned * tail], axis=0).astype(BF)
                qw_s[head, chunk, :CHUNK, :] = (growth * q.astype(F32)).astype(BF)
                side = jnp.concatenate(
                    [v[:, e * DV : (e + 1) * DV], (growth * k_wide).astype(BF)], axis=1
                )
                kept.append((head, chunk, side))
        for inverse, (head, chunk, side) in zip(unit_lower_inverses(mixes), kept):
            solved = mm(inverse.astype(BF), side)
            u_s[head, chunk] = solved[:, :DV]
            qw_s[head, chunk, CHUNK:, :] = solved[:, DV:].astype(BF)

    @pl.when(step == steps - 1)
    def scan():
        row = lax.broadcasted_iota(jnp.int32, (DK, DV + DK), 0)
        col = lax.broadcasted_iota(jnp.int32, (DK, DV + DK), 1)
        start = jnp.where(row + DV == col, 1.0, 0.0)
        for head in range(heads):
            state[head] = start

        @pl.loop(0, chunks)
        def advance(chunk):
            at = pl.ds(pl.multiple_of(chunk * CHUNK, CHUNK), CHUNK)
            firsts = [mm(qw_s[head, chunk], state[head].astype(BF)) for head in range(heads)]
            seconds = []
            for head, first in enumerate(firsts):
                lower = first[CHUNK:]
                u = jnp.concatenate([u_s[head, chunk] - lower[:, :DV], -lower[:, DV:]], axis=1)
                seconds.append(mm(at_s[head, chunk], u.astype(BF)))
            for head, (first, second) in enumerate(zip(firsts, seconds)):
                out = first[:CHUNK] + second[:CHUNK]
                core[at, head * DV : (head + 1) * DV] = out[:, :DV]
                linear[at, head * DK : (head + 1) * DK] = out[:, DV:].astype(BF)
                state[head] = closing[head, chunk] * state[head] + second[CHUNK:]


def delta_terms(x, w_query, w_key, w_value, w_zgate, cumulative, beta):
    tokens, width = x.shape
    heads = beta.shape[0]
    steps = heads // 2
    chunks = tokens // CHUNK
    closing = jnp.exp(cumulative[:, CHUNK - 1 :: CHUNK])
    rows = jnp.concatenate([cumulative.reshape(steps, 2, tokens), beta.reshape(steps, 2, tokens)], axis=1)
    cols = jnp.swapaxes(rows, 1, 2)
    flops = 2 * tokens * width * 6 * DK * steps + heads * chunks * 26 * 2 * 128**3
    return pl.pallas_call(
        delta_kernel,
        grid=(steps,),
        in_specs=[
            pl.BlockSpec(memory_space=pltpu.SMEM),
            pl.BlockSpec((tokens, width), lambda i: (0, 0)),
            pl.BlockSpec((width, DK), lambda i: (0, i)),
            pl.BlockSpec((width, DK), lambda i: (0, i)),
            pl.BlockSpec((width, 2 * DV), lambda i: (0, i)),
            pl.BlockSpec((width, 2 * DV), lambda i: (0, i)),
            pl.BlockSpec((1, tokens, 4), lambda i: (i, 0, 0)),
            pl.BlockSpec((1, 4, tokens), lambda i: (i, 0, 0)),
        ],
        out_specs=[
            pl.BlockSpec((tokens, 2 * DV), lambda i: (0, i)),
            pl.BlockSpec((tokens, heads * DV), lambda i: (0, 0)),
            pl.BlockSpec((tokens, heads * DK), lambda i: (0, 0)),
        ],
        out_shape=[
            jax.ShapeDtypeStruct((tokens, heads * DV), BF),
            jax.ShapeDtypeStruct((tokens, heads * DV), F32),
            jax.ShapeDtypeStruct((tokens, heads * DK), BF),
        ],
        scratch_shapes=[
            pltpu.VMEM((tokens, DK), BF),
            pltpu.VMEM((tokens, DK), BF),
            pltpu.VMEM((tokens, 2 * DV), BF),
            pltpu.VMEM((heads, chunks, 2 * CHUNK, DK), BF),
            pltpu.VMEM((heads, chunks, CHUNK + DK, CHUNK), BF),
            pltpu.VMEM((heads, chunks, CHUNK, DV), F32),
            pltpu.VMEM((heads, DK, DV + DK), F32),
        ],
        compiler_params=pltpu.CompilerParams(
            dimension_semantics=("arbitrary",), vmem_limit_bytes=56 * 2**20
        ),
        cost_estimate=pl.CostEstimate(flops=flops * 3, bytes_accessed=28 * 2**20, transcendentals=0),
    )(closing, x, w_query, w_key, w_value, w_zgate, cols, rows)


def compose_kernel(order, init, docs, out):
    slots, listed = order.shape

    def advance(j, carry):
        for slot in range(slots):
            doc = order[slot, j]
            state = out[slot]
            high = state.astype(BF)
            low = (state - high.astype(F32)).astype(BF)
            moved = mm(docs[doc, :DK, :], jnp.concatenate([high, low], axis=1))
            out[slot] = moved[:, :DV] + moved[:, DV:] + docs[doc, DK:, :].astype(F32)
        return carry

    for slot in range(slots):
        out[slot] = init[...]
    lax.fori_loop(0, listed, advance, 0)


def compose(order, init, docs):
    slots, listed = order.shape
    return pl.pallas_call(
        compose_kernel,
        in_specs=[
            pl.BlockSpec(memory_space=pltpu.SMEM),
            pl.BlockSpec(memory_space=pltpu.VMEM),
            pl.BlockSpec(memory_space=pltpu.VMEM),
        ],
        out_specs=pl.BlockSpec(memory_space=pltpu.VMEM),
        out_shape=jax.ShapeDtypeStruct((slots, DK, DV), F32),
        compiler_params=pltpu.CompilerParams(vmem_limit_bytes=24 * 2**20),
        cost_estimate=pl.CostEstimate(
            flops=slots * listed * 4 * 128**3 * 8, bytes_accessed=4 * 2**20, transcendentals=0
        ),
    )(order, init, docs)


def gate_kernel(half, core, linear, gate, start, gain, out):
    del half
    for head in range(start.shape[0]):
        at = slice(head * DV, (head + 1) * DV)
        state = start[head]
        high = state.astype(BF)
        low = (state - high.astype(F32)).astype(BF)
        moved = mm(linear[:, at], jnp.concatenate([high, low], axis=1))
        values = core[:, at] + moved[:, :DV] + moved[:, DV:]
        z = gate[:, at].astype(F32)
        mean = jnp.mean(values * values, axis=-1, keepdims=True)
        out[:, at] = (values * lax.rsqrt(mean + 1e-06) * gain[...] * (z * jax.nn.sigmoid(z))).astype(BF)


def gated(half, core, linear, gate, start, gain):
    tokens, width = core.shape
    tiles = tokens // 2 // ROWS
    block = pl.BlockSpec((ROWS, width), lambda i, half: (half[0] * tiles + i, 0))
    return pl.pallas_call(
        gate_kernel,
        grid_spec=pltpu.PrefetchScalarGridSpec(
            num_scalar_prefetch=1,
            grid=(tiles,),
            in_specs=[
                block,
                block,
                block,
                pl.BlockSpec(start.shape, lambda i, half: (0, 0, 0)),
                pl.BlockSpec((1, DV), lambda i, half: (0, 0)),
            ],
            out_specs=pl.BlockSpec((ROWS, width), lambda i, half: (i, 0)),
        ),
        out_shape=jax.ShapeDtypeStruct((tokens // 2, width), BF),
        compiler_params=pltpu.CompilerParams(
            dimension_semantics=("arbitrary",), vmem_limit_bytes=24 * 2**20
        ),
        cost_estimate=pl.CostEstimate(flops=2**30, bytes_accessed=5 * 2**20, transcendentals=0),
    )(half, core, linear, gate, start, gain)


def decays(x, w_gates, decay_log, dt_bias):
    heads = decay_log.shape[0]
    weights = jnp.concatenate([w_gates[0], w_gates[1]], axis=1)
    pre = lax.dot_general(weights, x, (((0,), (1,)), ((), ())), preferred_element_type=F32)
    pre = pre.astype(BF).astype(F32)
    beta = jax.nn.sigmoid(pre[heads:])
    logdecay = -jnp.exp(decay_log)[:, None] * jax.nn.softplus(pre[:heads] + dt_bias[:, None])
    parts = logdecay.reshape(heads, -1, CHUNK)
    position = jnp.arange(CHUNK)
    upper = (position[:, None] <= position[None, :]).astype(F32)
    cumulative = jnp.einsum("hct,ts->hcs", parts, upper, precision=lax.Precision.HIGHEST)
    return cumulative.reshape(heads, -1), beta


def on_device(
    tokens_in,
    w_query,
    w_key,
    w_value,
    w_zgate,
    w_gates,
    w_out,
    decay_log,
    dt_bias,
    norm_gain,
    init_state,
    doc_trans,
    doc_state,
    retrieval,
    doc_place,
    assignment,
):
    heads = decay_log.shape[0]
    store_count = lax.axis_size("store")
    copies = store_count // heads
    swap = [(0, 1), (1, 0)]
    docs = jnp.concatenate([doc_trans, doc_state], axis=2)
    if copies > 1:
        docs = jnp.repeat(docs, copies, axis=1)
    docs = lax.all_to_all(docs, "store", split_axis=1, concat_axis=0, tiled=True)[:, 0]
    x = lax.all_gather(tokens_in, "head", axis=0, tiled=True)
    other_out = lax.ppermute(w_out, "head", swap)
    cumulative, beta = decays(x, w_gates, decay_log, dt_bias)
    gate, core, linear = delta_terms(x, w_query, w_key, w_value, w_zgate, cumulative, beta)
    order = doc_place[retrieval[assignment]]
    my_head = lax.axis_index("store") // copies
    init = lax.dynamic_index_in_dim(init_state, my_head, 0, keepdims=False)
    states = compose(order, init, docs)
    start = lax.all_to_all(states, "store", split_axis=0, concat_axis=0, tiled=True)[::copies]
    half = lax.axis_index("head").astype(jnp.int32).reshape(1)
    gain = norm_gain.reshape(1, DV)
    away = gated(1 - half, core, linear, gate, start, gain)
    received = lax.ppermute(away, "head", swap)
    own = gated(half, core, linear, gate, start, gain)
    return (mm(own, w_out) + mm(received, other_out)).astype(BF)


def solution(mesh):
    in_specs = (
        P(("groups", "store", "head"), None),
        P(None, "head"),
        P(None, "head"),
        P(None, "head"),
        P(None, "head"),
        P(None, None, "head"),
        P("head", None),
        P("head"),
        P("head"),
        P(),
        P("head", None, None),
        P(("groups", "store"), "head", None, None),
        P(("groups", "store"), "head", None, None),
        P("groups", None),
        P("groups"),
        P("groups"),
    )
    out_specs = P(("groups", "store", "head"), None)
    return jax.shard_map(
        on_device, mesh=mesh, in_specs=in_specs, out_specs=out_specs, check_vma=False
    )
```

time: 443 us -> 157 us (0.35); the launches traced: 437 us -> 157 us
  matrix products: 267 us -> 11.8 us
  Pallas kernels: 0 us -> 59 us
  other arithmetic: 38 us -> 2.62 us
  local copies, waits for them, and re-layouts: 34.1 us -> 12.3 us
  waiting for transfers between devices: 66.2 us -> 46 us
  starting transfers between devices: 16.8 us -> 11.4 us
    dot_general x101 -> x4, matrix products: 267 us -> 11.8 us  [the longest x2 8.24 us: mm(): return jnp.dot(left, right, preferred_element_type=F32)]
    pallas_call x0 -> x4, Pallas kernels: none -> 59 us  [the longest x1 50.1 us: delta_terms(): pl.pallas_call(delta_kernel, grid=(steps,), in_specs=[pl.BlockSpec(memory...]
    reduce_scatter x1 -> x0, waiting for transfers between devices: 16 us -> none  [on_device(): lax.psum_scatter(jnp.dot(mixed_rows, w_out, preferred_element_type=jnp.fl...]
    gather x4 -> x3, local copies, waits for them, and re-layouts: 17.8 us -> 1.86 us  [on_device(): order = doc_place[retrieval[assignment]]]
    select_n x5 -> x2, other arithmetic: 15.1 us -> 0.01 us  [on_device(): order = doc_place[retrieval[assignment]]]
    convert_element_type x5 -> x0, other arithmetic: 8.15 us -> none  [the longest x1 3.83 us: on_device(): return lax.psum_scatter(jnp.dot(mixed_rows, w_out, preferred_element_type...]
    reduce_sum x6 -> x0, other arithmetic: 6.76 us -> none  [the longest x1 3.49 us: gated_mix(): jnp.mean(core_out * core_out, axis=-1, keepdims=True) + 1e-06]
    all_to_all x3 -> x2, starting transfers between devices: 16.7 us -> 11.2 us  [the longest x1 7.41 us: on_device(): lax.all_to_all(docs, 'store', split_axis=1, concat_axis=0, tiled=True)[:, 0]]
  transfers between devices with their start and end apart: 5 -> 5, of which waited for: 4 -> 1; matrix products, arithmetic and copies ran while one was open for 36% -> 7% of each run, Pallas kernels for 0% -> 38%
where the time goes in v1:
time: 157 us
  Pallas kernels  59 us (38%)
  waiting for transfers between devices  46 us (29%)
  between operations  13.7 us (9%)
  local copies, waits for them, and re-layouts  12.3 us (8%)
  matrix products  11.8 us (8%)
  starting transfers between devices  11.4 us (7%)
  other arithmetic  2.62 us (2%)
    pallas_call x1, Pallas kernels, delta_terms(): pl.pallas_call(delta_kernel, grid=(steps,), in_specs=[pl.BlockSpec(memory...  50.1 us
    all_to_all x1, waiting for transfers between devices, on_device(): lax.all_to_all(docs, 'store', split_axis=1, concat_axis=0, tiled=True)[:, 0]  45.3 us
    dot_general x2, matrix products, mm(): return jnp.dot(left, right, preferred_element_type=F32)  8.24 us
    all_to_all x1, starting transfers between devices, on_device(): lax.all_to_all(docs, 'store', split_axis=1, concat_axis=0, tiled=True)[:, 0]  7.41 us
    pallas_call x1, Pallas kernels, compose(): pl.pallas_call(compose_kernel, in_specs=[pl.BlockSpec(memory_space=pltpu....  6.12 us
    unnamed x25, local copies, waits for them, and re-layouts  6.08 us
    all_to_all x1, starting transfers between devices, on_device(): lax.all_to_all(states, 'store', split_axis=0, concat_axis=0, tiled=True)  3.77 us
    dot_general x1, matrix products, decays(): lax.dot_general(weights, x, (((0,), (1,)), ((), ())), preferred_element_t...  3.37 us
  transfers between devices with their start and end apart: 5, of which 1 were waited for; matrix products, arithmetic and copies ran while one was open for 7% of the time, Pallas kernels for 38%

profile of v1, /device:TPU:0, one launch (start us, length us, event | category | flops | bytes accessed | tf_op | source)
XLA Modules:
  0.0 156.7 jit_solution(16346807529255482520)
XLA Ops:
  6.5 0.0 copy-start
  6.5 1.8 %pad_maximum_fusion = bf16[4,8,256,128]{3,2,1,0:T(8,128)(2,1)S(1)} fusion(bf16[4,8,128,128]{3,2,1,0:T(8,128)(2,1)} %param.28, bf16[4,8,128,128]{3,2,1,0:T(8,128)(2,1)} %param.27), kind=kLoop, calls=%fused_computation.3 | loop fusion | flops 4194304 | bytes 4194304 | tf_op jit(solution)/shard_map/concatenate | solution.py:294
  8.4 1.5 copy.27
  9.9 0.0 copy-start.10
  9.9 0.0 copy-start.6
  9.9 0.0 copy-start.5
  9.9 7.4 %all-to-all-start = ((bf16[4,8,256,128]{3,2,0,1:T(8,128)(2,1)}), bf16[4,8,256,128]{3,2,0,1:T(8,128)(2,1)S(1)}, u32[]{:S(2)}, u32[]{:S(2)}) async-start(bf16[4,8,256,128]{3,2,0,1:T(8,128)(2,1)} %copy.27), calls=%async_computation | async-start | bytes 4194304 | tf_op jit(solution)/shard_map/all_to_all | solution.py:297
  17.3 0.0 copy-start.11
  17.3 0.0 copy-start.7
  17.3 0.0 all-gather.2.cloned.1.call-start
  17.4 0.7 all-gather.2.cloned.1.call-update
  18.1 0.1 collective-permute-start.1
  18.2 0.0 copy-done.10
  18.2 0.0 copy-done.6
  18.2 0.6 gather_fusion
  18.8 0.1 reshape.47
  18.9 0.0 copy-done.5
  18.9 1.2 gather_fusion.1
  20.1 0.1 reshape.46.order
  20.2 0.0 copy-done
  20.2 0.0 copy-done.11
  20.2 0.0 copy-done.7
  20.3 45.3 %all-to-all-done = bf16[4,8,256,128]{3,2,0,1:T(8,128)(2,1)S(1)} async-done(((bf16[4,8,256,128]{3,2,0,1:T(8,128)(2,1)}), bf16[4,8,256,128]{3,2,0,1:T(8,128)(2,1)S(1)}, u32[]{:S(2)}, u32[]{:S(2)}) %all-to-all-start) | async-done | bytes 2097184 | tf_op jit(solution)/shard_map/all_to_all | solution.py:297
  65.6 6.1 %shard_map.155 = f32[8,128,128]{2,1,0:T(8,128)} custom-call(s32[8,16]{1,0:T(8,128)S(1)} %reshape.46.order, f32[128,128]{1,0:T(8,128)S(1)} %dynamic-slice_bitcast_fusion.init, bf16[32,256,128]{2,1,0:T(8,128)(2,1)S(1)} %bitcast.33), custom_call_target="tpu_custom_call" | custom-call | flops 8589934592 | bytes 4194304 | tf_op jit(solution)/shard_map/pallas_call | solution.py:202
  71.7 0.0 copy-start.8
  71.7 3.8 %all-to-all-start.1 = ((f32[8,128,128]{2,1,0:T(8,128)}), f32[8,128,128]{2,1,0:T(8,128)S(1)}, u32[]{:S(2)}, u32[]{:S(2)}) async-start(f32[8,128,128]{2,1,0:T(8,128)} %shard_map.155), calls=%async_computation.1 | async-start | bytes 1048576 | tf_op jit(solution)/shard_map/all_to_all | solution.py:306
  75.5 0.0 all-gather.2.cloned.1.call-done.x
  75.5 3.4 %fusion = f32[16,1024]{1,0:T(8,128)S(1)} fusion(bf16[1024,2048]{1,0:T(8,128)(2,1)} %all-gather.2.cloned.1.call-done.x, bf16[2048,8]{0,1:T(8,128)(2,1)S(1)} %get-tuple-element.16, bf16[2048,8]{0,1:T(8,128)(2,1)S(1)} %get-tuple-element.15), kind=kOutput, calls=%fused_computation.5 | convolution fusion | flops 67272704 | bytes 4325376 | tf_op jit(solution)/shard_map/dot_general | solution.py:261
  78.9 0.0 copy-done.8
  78.9 0.1 fusion.11
  79.0 0.2 fusion.5
  79.2 0.7 pad_maximum_fusion.1
  79.9 2.0 %copy.24.cols = f32[4,1024,4]{2,1,0:T(8,128)} copy(f32[4,1024,4]{1,2,0:T(4,128)S(1)} %get-tuple-element.12) | data formatting | bytes 131072 | tf_op jit(solution)/shard_map/transpose | solution.py:141
  81.8 0.1 slice.18
  81.9 0.6 exp.15.closing
  82.6 0.0 copy-start.4
  82.6 50.1 %shard_map.154 = (bf16[1024,1024]{1,0:T(8,128)(2,1)}, f32[1024,1024]{1,0:T(8,128)}, bf16[1024,1024]{1,0:T(8,128)(2,1)}) custom-call(f32[8,8]{1,0:T(8,128)} %exp.15.closing, bf16[1024,2048]{1,0:T(8,128)(2,1)} %all-gather.2.cloned.1.call-done.x, bf16[2048,512]{1,0:T(8,128)(2,1)} %w_q.1, bf16[2048,512]{1,0:T(8,128)(2,1)} %w_k.1, bf16[2048,1024]{1,0:T(8,128)(2,1)} %w_v.1, ...), custom_call_target="tpu_custom_call" | custom-call | flops 59592671232 | bytes 29360128 | tf_op jit(solution)/shard_map/pallas_call | solution.py:143
  132.6 0.0 all-to-all-done.1.start
  132.7 0.0 copy-done.4
  132.7 0.0 copy-start.1
  132.7 2.2 %copy-done.1 = f32[1024,1024]{1,0:T(8,128)S(1)} copy-done((f32[1024,1024]{1,0:T(8,128)S(1)}, f32[1024,1024]{1,0:T(8,128)}, u32[]{:S(2)}) %copy-start.1) | copy-done | bytes 4194328
  134.8 0.0 copy-start.2
  134.9 1.6 %copy-done.2 = bf16[1024,1024]{1,0:T(8,128)(2,1)S(1)} copy-done((bf16[1024,1024]{1,0:T(8,128)(2,1)S(1)}, bf16[1024,1024]{1,0:T(8,128)(2,1)}, u32[]{:S(2)}) %copy-start.2) | copy-done | bytes 2097176
  136.4 0.0 copy-start.3
  136.4 1.6 %copy-done.3 = bf16[1024,1024]{1,0:T(8,128)(2,1)S(1)} copy-done((bf16[1024,1024]{1,0:T(8,128)(2,1)S(1)}, bf16[1024,1024]{1,0:T(8,128)(2,1)}, u32[]{:S(2)}) %copy-start.3) | copy-done | bytes 2097176
  138.0 1.4 shard_map.157
  139.4 0.0 copy-start.9
  139.5 0.1 collective-permute-start
  139.5 1.4 shard_map.156
  141.0 0.7 copy-done.9
  141.6 2.4 %fusion.15 = f32[512,2048]{1,0:T(8,128)S(1)} fusion(bf16[512,1024]{1,0:T(8,128)(2,1)S(1)} %shard_map.156, bf16[1024,2048]{1,0:T(8,128)(2,1)S(1)} %copy-done.9), kind=kOutput, calls=%fused_computation.33 | convolution fusion | flops 2147483648 | bytes 9437184 | tf_op jit(solution)/shard_map/dot_general | solution.py:17
  144.0 0.0 collective-permute-done.1
  144.0 0.0 collective-permute-done
  144.0 5.9 %add_convert_fusion = bf16[512,2048]{1,0:T(8,128)(2,1)} fusion(f32[512,2048]{1,0:T(8,128)S(1)} %fusion.15, bf16[512,1024]{1,0:T(8,128)(2,1)S(1)} %collective-permute-done, bf16[1024,2048]{1,0:T(8,128)(2,1)} %collective-permute-done.1), kind=kOutput, calls=%fused_computation.2 | convolution fusion | flops 2149580800 | bytes 11534336 | tf_op jit(solution)/shard_map/dot_general | solution.py:17
  (10 shorter events, 0.1 us)
Async XLA Ops:
  6.5 13.7 %copy-start = (f32[8,128,128]{2,1,0:T(8,128)S(1)}, f32[8,128,128]{2,1,0:T(8,128)}, u32[]{:S(2)}) copy-start(f32[8,128,128]{2,1,0:T(8,128)} %param.26) | copy-start | bytes 1572868
  9.9 8.3 %copy-start.10 = (s32[8]{0:T(128)S(1)}, s32[8]{0:T(128)}, u32[]{:S(2)}) copy-start(s32[8]{0:T(128)} %param.31) | copy-start | bytes 100
  9.9 8.3 %copy-start.6 = (s32[8,16]{1,0:T(8,128)S(1)}, s32[8,16]{1,0:T(8,128)}, u32[]{:S(2)}) copy-start(s32[8,16]{1,0:T(8,128)} %param.29) | copy-start | bytes 1540
  9.9 9.0 %copy-start.5 = (s32[32]{0:T(128)S(1)}, s32[32]{0:T(128)}, u32[]{:S(2)}) copy-start(s32[32]{0:T(128)} %param.30) | copy-start | bytes 388
  9.9 55.7 %all-to-all-start = ((bf16[4,8,256,128]{3,2,0,1:T(8,128)(2,1)}), bf16[4,8,256,128]{3,2,0,1:T(8,128)(2,1)S(1)}, u32[]{:S(2)}, u32[]{:S(2)}) async-start(bf16[4,8,256,128]{3,2,0,1:T(8,128)(2,1)} %copy.27), calls=%async_computation | async-start | bytes 4194304 | tf_op jit(solution)/shard_map/all_to_all | solution.py:297
  17.3 2.9 %copy-start.11 = (f32[8]{0:T(128)S(1)}, f32[8]{0:T(128)}, u32[]{:S(2)}) copy-start(f32[8]{0:T(128)} %param.23) | copy-start | bytes 100
  17.3 2.9 %copy-start.7 = (bf16[2,2048,8]{1,2,0:T(8,128)(2,1)S(1)}, bf16[2,2048,8]{1,2,0:T(8,128)(2,1)}, u32[]{:S(2)}) copy-start(bf16[2,2048,8]{1,2,0:T(8,128)(2,1)} %param.21) | copy-start | bytes 196612
  17.3 58.1 %all-gather.2.cloned.1.call-start = ((), (), s32[]{:S(2)}) async-start(), calls=%async_computation.2 | async-start | bytes 6291456 | tf_op jit(solution)/shard_map/all_gather | solution.py:298
  18.1 125.9 %collective-permute-start.1 = (bf16[1024,2048]{1,0:T(8,128)(2,1)}, bf16[1024,2048]{1,0:T(8,128)(2,1)}, u32[]{:S(2)}, u32[]{:S(2)}) collective-permute-start(bf16[1024,2048]{1,0:T(8,128)(2,1)} %param.22), channel_id=1, source_target_pairs={{0,1},{1,0},{2,3},{3,2},{4,5},{5,4},{6,7},{7,6},{8,9},{9,8},{10,11... | collective-permute-start | bytes 12582920 | tf_op jit(solution)/shard_map/ppermute | solution.py:299
  71.7 7.2 %copy-start.8 = (f32[8]{0:T(128)S(1)}, f32[8]{0:T(128)}, u32[]{:S(2)}) copy-start(f32[8]{0:T(128)} %param.24) | copy-start | bytes 100
  71.7 61.0 %all-to-all-start.1 = ((f32[8,128,128]{2,1,0:T(8,128)}), f32[8,128,128]{2,1,0:T(8,128)S(1)}, u32[]{:S(2)}, u32[]{:S(2)}) async-start(f32[8,128,128]{2,1,0:T(8,128)} %shard_map.155), calls=%async_computation.1 | async-start | bytes 1048576 | tf_op jit(solution)/shard_map/all_to_all | solution.py:306
  82.6 50.1 %copy-start.4 = (f32[128]{0:T(128)S(1)}, f32[128]{0:T(128)}, u32[]{:S(2)}) copy-start(f32[128]{0:T(128)} %param.25) | copy-start | bytes 1540
  132.7 2.2 %copy-start.1 = (f32[1024,1024]{1,0:T(8,128)S(1)}, f32[1024,1024]{1,0:T(8,128)}, u32[]{:S(2)}) copy-start(f32[1024,1024]{1,0:T(8,128)} %get-tuple-element.8.core) | copy-start | bytes 12582916
  134.8 1.6 %copy-start.2 = (bf16[1024,1024]{1,0:T(8,128)(2,1)S(1)}, bf16[1024,1024]{1,0:T(8,128)(2,1)}, u32[]{:S(2)}) copy-start(bf16[1024,1024]{1,0:T(8,128)(2,1)} %get-tuple-element.10.gate) | copy-start | bytes 6291460
  136.4 1.6 %copy-start.3 = (bf16[1024,1024]{1,0:T(8,128)(2,1)S(1)}, bf16[1024,1024]{1,0:T(8,128)(2,1)}, u32[]{:S(2)}) copy-start(bf16[1024,1024]{1,0:T(8,128)(2,1)} %get-tuple-element.9.linear) | copy-start | bytes 6291460
  139.4 2.2 %copy-start.9 = (bf16[1024,2048]{1,0:T(8,128)(2,1)S(1)}, bf16[1024,2048]{1,0:T(8,128)(2,1)}, u32[]{:S(2)}) copy-start(bf16[1024,2048]{1,0:T(8,128)(2,1)} %param.22) | copy-start | bytes 12582916
  139.5 4.6 %collective-permute-start = (bf16[512,1024]{1,0:T(8,128)(2,1)S(1)}, bf16[512,1024]{1,0:T(8,128)(2,1)S(1)}, u32[]{:S(2)}, u32[]{:S(2)}) collective-permute-start(bf16[512,1024]{1,0:T(8,128)(2,1)S(1)} %shard_map.157), channel_id=1, source_target_pairs={{0,1},{1,0},{2,3},{3,2},{4,5},{5,4},{6,7},{7,6},{8,9},{9,8},{10,11... | collective-permute-start | bytes 3145736 | tf_op jit(solution)/shard_map/ppermute | solution.py:310
Sparse Core Ops, SparseCore 0:
  19.7 15.0 all-gather.1

commit v2 on v1

--- a/solution.py
+++ b/solution.py
@@ -48,27 +48,26 @@
     return inverses
 
 
-def delta_kernel(
-    closing, x, w_q, w_k, w_v, w_z, cols, rows, gate, core, linear, q_s, k_s, v_s, qw_s, at_s, u_s, state
-):
-    step = pl.program_id(0)
-    steps = pl.num_programs(0)
-    tokens = x.shape[0]
-    chunks = tokens // CHUNK
-    heads = core.shape[1] // DV
-
-    @pl.loop(0, tokens // ROWS)
+def terms_kernel(half, x, other, w_q, w_k, w_v, w_z, cols, rows, gate, qw, at_out, u_out, w_s, q_s, k_s, v_s):
+    held = x.shape[0]
+    chunks = 2 * held // CHUNK
+    w_s[:, :DK] = w_q[...]
+    w_s[:, DK:] = w_k[...]
+
+    @pl.loop(0, held // ROWS)
     def project(tile):
-        at = pl.ds(pl.multiple_of(tile * ROWS, ROWS), ROWS)
-        part = x[at, :]
-        q = mm(part, w_q[...]).astype(BF).astype(F32)
-        q_s[at, :] = (
-            q * lax.rsqrt(jnp.sum(q * q, axis=-1, keepdims=True) + 1e-06) * DK ** (-0.5)
-        ).astype(BF)
-        k = mm(part, w_k[...]).astype(BF).astype(F32)
-        k_s[at, :] = (k * lax.rsqrt(jnp.sum(k * k, axis=-1, keepdims=True) + 1e-06)).astype(BF)
-        v_s[at, :] = mm(part, w_v[...]).astype(BF)
-        gate[at, :] = mm(part, w_z[...]).astype(BF)
+        source = pl.ds(pl.multiple_of(tile * ROWS, ROWS), ROWS)
+        for tokens, place in ((x, half[0]), (other, 1 - half[0])):
+            at = pl.ds(pl.multiple_of(place * held + tile * ROWS, ROWS), ROWS)
+            part = tokens[source, :]
+            both = mm(part, w_s[...]).astype(BF).astype(F32)
+            q, k = both[:, :DK], both[:, DK:]
+            q_s[at, :] = (
+                q * lax.rsqrt(jnp.sum(q * q, axis=-1, keepdims=True) + 1e-06) * DK ** (-0.5)
+            ).astype(BF)
+            k_s[at, :] = (k * lax.rsqrt(jnp.sum(k * k, axis=-1, keepdims=True) + 1e-06)).astype(BF)
+            v_s[at, :] = mm(part, w_v[...]).astype(BF)
+            gate[at, :] = mm(part, w_z[...]).astype(BF)
 
     group = min(4, chunks)
 
@@ -95,57 +94,34 @@
                 attend = jnp.where(row >= col, decay * both[CHUNK:], 0.0)
                 growth = jnp.exp(cum_c)
                 tail = jnp.exp(cum_r[:, CHUNK - 1 :] - cum_r) * beta_r
-                head = 2 * step + e
-                at_s[head, chunk] = jnp.concatenate([attend, k_turned * tail], axis=0).astype(BF)
-                qw_s[head, chunk, :CHUNK, :] = (growth * q.astype(F32)).astype(BF)
+                at_out[e, chunk] = jnp.concatenate([attend, k_turned * tail], axis=0).astype(BF)
+                qw[e, chunk, :CHUNK, :] = (growth * q.astype(F32)).astype(BF)
                 side = jnp.concatenate(
                     [v[:, e * DV : (e + 1) * DV], (growth * k_wide).astype(BF)], axis=1
                 )
-                kept.append((head, chunk, side))
-        for inverse, (head, chunk, side) in zip(unit_lower_inverses(mixes), kept):
+                kept.append((e, chunk, side))
+        for inverse, (e, chunk, side) in zip(unit_lower_inverses(mixes), kept):
             solved = mm(inverse.astype(BF), side)
-            u_s[head, chunk] = solved[:, :DV]
-            qw_s[head, chunk, CHUNK:, :] = solved[:, DV:].astype(BF)
-
-    @pl.when(step == steps - 1)
-    def scan():
-        row = lax.broadcasted_iota(jnp.int32, (DK, DV + DK), 0)
-        col = lax.broadcasted_iota(jnp.int32, (DK, DV + DK), 1)
-        start = jnp.where(row + DV == col, 1.0, 0.0)
-        for head in range(heads):
-            state[head] = start
-
-        @pl.loop(0, chunks)
-        def advance(chunk):
-            at = pl.ds(pl.multiple_of(chunk * CHUNK, CHUNK), CHUNK)
-            firsts = [mm(qw_s[head, chunk], state[head].astype(BF)) for head in range(heads)]
-            seconds = []
-            for head, first in enumerate(firsts):
-                lower = first[CHUNK:]
-                u = jnp.concatenate([u_s[head, chunk] - lower[:, :DV], -lower[:, DV:]], axis=1)
-                seconds.append(mm(at_s[head, chunk], u.astype(BF)))
-            for head, (first, second) in enumerate(zip(firsts, seconds)):
-                out = first[:CHUNK] + second[:CHUNK]
-                core[at, head * DV : (head + 1) * DV] = out[:, :DV]
-                linear[at, head * DK : (head + 1) * DK] = out[:, DV:].astype(BF)
-                state[head] = closing[head, chunk] * state[head] + second[CHUNK:]
-
-
-def delta_terms(x, w_query, w_key, w_value, w_zgate, cumulative, beta):
-    tokens, width = x.shape
+            u_out[e, chunk] = solved[:, :DV]
+            qw[e, chunk, CHUNK:, :] = solved[:, DV:].astype(BF)
+
+
+def chunk_terms(half, x, other, w_query, w_key, w_value, w_zgate, cumulative, beta):
+    held, width = x.shape
+    tokens = 2 * held
     heads = beta.shape[0]
     steps = heads // 2
     chunks = tokens // CHUNK
-    closing = jnp.exp(cumulative[:, CHUNK - 1 :: CHUNK])
     rows = jnp.concatenate([cumulative.reshape(steps, 2, tokens), beta.reshape(steps, 2, tokens)], axis=1)
     cols = jnp.swapaxes(rows, 1, 2)
     flops = 2 * tokens * width * 6 * DK * steps + heads * chunks * 26 * 2 * 128**3
     return pl.pallas_call(
-        delta_kernel,
+        terms_kernel,
         grid=(steps,),
         in_specs=[
             pl.BlockSpec(memory_space=pltpu.SMEM),
-            pl.BlockSpec((tokens, width), lambda i: (0, 0)),
+            pl.BlockSpec((held, width), lambda i: (0, 0)),
+            pl.BlockSpec((held, width), lambda i: (0, 0)),
             pl.BlockSpec((width, DK), lambda i: (0, i)),
             pl.BlockSpec((width, DK), lambda i: (0, i)),
             pl.BlockSpec((width, 2 * DV), lambda i: (0, i)),
@@ -155,28 +131,82 @@
         ],
         out_specs=[
             pl.BlockSpec((tokens, 2 * DV), lambda i: (0, i)),
-            pl.BlockSpec((tokens, heads * DV), lambda i: (0, 0)),
-            pl.BlockSpec((tokens, heads * DK), lambda i: (0, 0)),
+            pl.BlockSpec((2, chunks, 2 * CHUNK, DK), lambda i: (i, 0, 0, 0)),
+            pl.BlockSpec((2, chunks, CHUNK + DK, CHUNK), lambda i: (i, 0, 0, 0)),
+            pl.BlockSpec((2, chunks, CHUNK, DV), lambda i: (i, 0, 0, 0)),
         ],
         out_shape=[
             jax.ShapeDtypeStruct((tokens, heads * DV), BF),
-            jax.ShapeDtypeStruct((tokens, heads * DV), F32),
-            jax.ShapeDtypeStruct((tokens, heads * DK), BF),
+            jax.ShapeDtypeStruct((heads, chunks, 2 * CHUNK, DK), BF),
+            jax.ShapeDtypeStruct((heads, chunks, CHUNK + DK, CHUNK), BF),
+            jax.ShapeDtypeStruct((heads, chunks, CHUNK, DV), F32),
         ],
         scratch_shapes=[
+            pltpu.VMEM((width, 2 * DK), BF),
             pltpu.VMEM((tokens, DK), BF),
             pltpu.VMEM((tokens, DK), BF),
             pltpu.VMEM((tokens, 2 * DV), BF),
-            pltpu.VMEM((heads, chunks, 2 * CHUNK, DK), BF),
-            pltpu.VMEM((heads, chunks, CHUNK + DK, CHUNK), BF),
-            pltpu.VMEM((heads, chunks, CHUNK, DV), F32),
-            pltpu.VMEM((heads, DK, DV + DK), F32),
         ],
         compiler_params=pltpu.CompilerParams(
             dimension_semantics=("arbitrary",), vmem_limit_bytes=56 * 2**20
         ),
         cost_estimate=pl.CostEstimate(flops=flops * 3, bytes_accessed=28 * 2**20, transcendentals=0),
-    )(closing, x, w_query, w_key, w_value, w_zgate, cols, rows)
+    )(half, x, other, w_query, w_key, w_value, w_zgate, cols, rows)
+
+
+def scan_kernel(closing, qw, at_in, u_in, core, linear, state):
+    heads = qw.shape[0]
+    chunk = pl.program_id(0)
+
+    @pl.when(chunk == 0)
+    def begin():
+        row = lax.broadcasted_iota(jnp.int32, (DK, DV + DK), 0)
+        col = lax.broadcasted_iota(jnp.int32, (DK, DV + DK), 1)
+        start = jnp.where(row + DV == col, 1.0, 0.0)
+        for head in range(heads):
+            state[head] = start
+
+    firsts = [mm(qw[head, 0], state[head].astype(BF)) for head in range(heads)]
+    seconds = []
+    for head, first in enumerate(firsts):
+        lower = first[CHUNK:]
+        u = jnp.concatenate([u_in[head, 0] - lower[:, :DV], -lower[:, DV:]], axis=1)
+        seconds.append(mm(at_in[head, 0], u.astype(BF)))
+    for head, (first, second) in enumerate(zip(firsts, seconds)):
+        out = first[:CHUNK] + second[:CHUNK]
+        core[:, head * DV : (head + 1) * DV] = out[:, :DV]
+        linear[:, head * DK : (head + 1) * DK] = out[:, DV:].astype(BF)
+        state[head] = closing[head, chunk] * state[head] + second[CHUNK:]
+
+
+def scan_chunks(closing, qw, attend, u):
+    heads, chunks = closing.shape
+    tokens = chunks * CHUNK
+    return pl.pallas_call(
+        scan_kernel,
+        grid=(chunks,),
+        in_specs=[
+            pl.BlockSpec(memory_space=pltpu.SMEM),
+            pl.BlockSpec((heads, 1, 2 * CHUNK, DK), lambda c: (0, c, 0, 0)),
+            pl.BlockSpec((heads, 1, CHUNK + DK, CHUNK), lambda c: (0, c, 0, 0)),
+            pl.BlockSpec((heads, 1, CHUNK, DV), lambda c: (0, c, 0, 0)),
+        ],
+        out_specs=[
+            pl.BlockSpec((CHUNK, heads * DV), lambda c: (c, 0)),
+            pl.BlockSpec((CHUNK, heads * DK), lambda c: (c, 0)),
+        ],
+        out_shape=[
+            jax.ShapeDtypeStruct((tokens, heads * DV), F32),
+            jax.ShapeDtypeStruct((tokens, heads * DK), BF),
+        ],
+        scratch_shapes=[pltpu.VMEM((heads, DK, DV + DK), F32)],
+        compiler_params=pltpu.CompilerParams(
+            dimension_semantics=("arbitrary",), vmem_limit_bytes=56 * 2**20
+        ),
+        cost_estimate=pl.CostEstimate(
+            flops=heads * chunks * 32 * 128**3, bytes_accessed=18 * 2**20, transcendentals=0
+        ),
+    )(closing, qw, attend, u)
 
 
 def compose_kernel(order, init, docs, out):
@@ -249,16 +279,47 @@
         ),
         out_shape=jax.ShapeDtypeStruct((tokens // 2, width), BF),
         compiler_params=pltpu.CompilerParams(
-            dimension_semantics=("arbitrary",), vmem_limit_bytes=24 * 2**20
+            dimension_semantics=("arbitrary",), vmem_limit_bytes=56 * 2**20
         ),
         cost_estimate=pl.CostEstimate(flops=2**30, bytes_accessed=5 * 2**20, transcendentals=0),
     )(half, core, linear, gate, start, gain)
 
 
-def decays(x, w_gates, decay_log, dt_bias):
+def project_kernel(own, received, w_own, w_other, out):
+    out[...] = (mm(own[...], w_own[...]) + mm(received[...], w_other[...])).astype(BF)
+
+
+def project_out(own, received, w_own, w_other):
+    tokens, depth = own.shape
+    width = w_own.shape[1]
+    tile = 256
+    left = pl.BlockSpec((tokens, depth), lambda i: (0, 0))
+    right = pl.BlockSpec((depth, tile), lambda i: (0, i))
+    return pl.pallas_call(
+        project_kernel,
+        grid=(width // tile,),
+        in_specs=[left, left, right, right],
+        out_specs=pl.BlockSpec((tokens, tile), lambda i: (0, i)),
+        out_shape=jax.ShapeDtypeStruct((tokens, width), BF),
+        compiler_params=pltpu.CompilerParams(
+            dimension_semantics=("arbitrary",), vmem_limit_bytes=56 * 2**20
+        ),
+        cost_estimate=pl.CostEstimate(
+            flops=4 * tokens * depth * width, bytes_accessed=12 * 2**20, transcendentals=0
+        ),
+    )(own, received, w_own, w_other)
+
+
+def decays(half, x, other, w_gates, decay_log, dt_bias):
     heads = decay_log.shape[0]
     weights = jnp.concatenate([w_gates[0], w_gates[1]], axis=1)
-    pre = lax.dot_general(weights, x, (((0,), (1,)), ((), ())), preferred_element_type=F32)
+    mine, theirs = (
+        lax.dot_general(weights, part, (((0,), (1,)), ((), ())), preferred_element_type=F32)
+        for part in (x, other)
+    )
+    pre = jnp.where(
+        half[0] == 0, jnp.concatenate([mine, theirs], axis=1), jnp.concatenate([theirs, mine], axis=1)
+    )
     pre = pre.astype(BF).astype(F32)
     beta = jax.nn.sigmoid(pre[heads:])
     logdecay = -jnp.exp(decay_log)[:, None] * jax.nn.softplus(pre[:heads] + dt_bias[:, None])
@@ -295,21 +356,27 @@
     if copies > 1:
         docs = jnp.repeat(docs, copies, axis=1)
     docs = lax.all_to_all(docs, "store", split_axis=1, concat_axis=0, tiled=True)[:, 0]
-    x = lax.all_gather(tokens_in, "head", axis=0, tiled=True)
+    other = lax.ppermute(tokens_in, "head", swap)
     other_out = lax.ppermute(w_out, "head", swap)
-    cumulative, beta = decays(x, w_gates, decay_log, dt_bias)
-    gate, core, linear = delta_terms(x, w_query, w_key, w_value, w_zgate, cumulative, beta)
+    half = lax.axis_index("head").astype(jnp.int32).reshape(1)
+    cumulative, beta = decays(half, tokens_in, other, w_gates, decay_log, dt_bias)
+    closing = jnp.exp(cumulative[:, CHUNK - 1 :: CHUNK])
+    gate, qw, attend, u = chunk_terms(
+        half, tokens_in, other, w_query, w_key, w_value, w_zgate, cumulative, beta
+    )
     order = doc_place[retrieval[assignment]]
     my_head = lax.axis_index("store") // copies
     init = lax.dynamic_index_in_dim(init_state, my_head, 0, keepdims=False)
+    init, order, closing, u = lax.optimization_barrier((init, order, closing, u))
     states = compose(order, init, docs)
+    states, closing = lax.optimization_barrier((states, closing))
     start = lax.all_to_all(states, "store", split_axis=0, concat_axis=0, tiled=True)[::copies]
-    half = lax.axis_index("head").astype(jnp.int32).reshape(1)
+    core, linear = scan_chunks(closing, qw, attend, u)
     gain = norm_gain.reshape(1, DV)
     away = gated(1 - half, core, linear, gate, start, gain)
     received = lax.ppermute(away, "head", swap)
     own = gated(half, core, linear, gate, start, gain)
-    return (mm(own, w_out) + mm(received, other_out)).astype(BF)
+    return project_out(own, received, w_out, other_out)
 
 
 def solution(mesh):

time: 157 us -> 108 us (0.69)
  waiting for transfers between devices: 46 us -> 4.06 us
  Pallas kernels: 59 us -> 74.7 us
  between operations: 13.7 us -> 0.18 us
  matrix products: 11.8 us -> 4.66 us
  local copies, waits for them, and re-layouts: 12.3 us -> 8.04 us
  starting transfers between devices: 11.4 us -> 13.5 us
    all_to_all x1, waiting for transfers between devices: 45.3 us -> 0.01 us  [on_device(): lax.all_to_all(docs, 'store', split_axis=1, concat_axis=0, tiled=True)[:, 0]]
    pallas_call x1 -> x3, Pallas kernels: 50.1 us -> 60.4 us  [the longest x1 38.9 us: chunk_terms(): pl.pallas_call(terms_kernel, grid=(steps,), in_specs=[pl.BlockSpec(memory...]
    dot_general x3 -> x2, matrix products: 11.6 us -> 4.49 us  [decays(): lax.dot_general(weights, part, (((0,), (1,)), ((), ())), preferred_elemen...]
    pallas_call x2, Pallas kernels: 2.82 us -> 8.21 us  [gated(): pl.pallas_call(gate_kernel, grid_spec=pltpu.PrefetchScalarGridSpec(num_sc...]
    unnamed x25 -> x19, local copies, waits for them, and re-layouts: 6.08 us -> 1.81 us
    all_to_all x1, waiting for transfers between devices: 0.01 us -> 4.05 us  [on_device(): lax.all_to_all(states, 'store', split_axis=0, concat_axis=0, tiled=True)]
    all_to_all x1, starting transfers between devices: 3.77 us -> 5.85 us  [on_device(): lax.all_to_all(states, 'store', split_axis=0, concat_axis=0, tiled=True)]
  transfers between devices with their start and end apart: 5 -> 5, of which waited for: 1 -> 1; matrix products, arithmetic and copies ran while one was open for 7% -> 13% of each run, Pallas kernels for 38% -> 60%
where the time goes in v2:
time: 108 us
  Pallas kernels  74.7 us (69%)
  starting transfers between devices  13.5 us (12%)
  local copies, waits for them, and re-layouts  8.04 us (7%)
  matrix products  4.66 us (4%)
  waiting for transfers between devices  4.06 us (4%)
  other arithmetic  2.57 us (2%)
    pallas_call x1, Pallas kernels, chunk_terms(): pl.pallas_call(terms_kernel, grid=(steps,), in_specs=[pl.BlockSpec(memory...  38.9 us
    pallas_call x1, Pallas kernels, scan_chunks(): pl.pallas_call(scan_kernel, grid=(chunks,), in_specs=[pl.BlockSpec(memory...  11.1 us
    pallas_call x1, Pallas kernels, project_out(): pl.pallas_call(project_kernel, grid=(width // tile,), in_specs=[left, lef...  10.4 us
    pallas_call x2, Pallas kernels, gated(): pl.pallas_call(gate_kernel, grid_spec=pltpu.PrefetchScalarGridSpec(num_sc...  8.21 us
    all_to_all x1, starting transfers between devices, on_device(): lax.all_to_all(docs, 'store', split_axis=1, concat_axis=0, tiled=True)[:, 0]  7.03 us
    pallas_call x1, Pallas kernels, compose(): pl.pallas_call(compose_kernel, in_specs=[pl.BlockSpec(memory_space=pltpu....  6.1 us
    all_to_all x1, starting transfers between devices, on_device(): lax.all_to_all(states, 'store', split_axis=0, concat_axis=0, tiled=True)  5.85 us
    dot_general x2, matrix products, decays(): lax.dot_general(weights, part, (((0,), (1,)), ((), ())), preferred_elemen...  4.49 us
  transfers between devices with their start and end apart: 5, of which 1 were waited for; matrix products, arithmetic and copies ran while one was open for 13% of the time, Pallas kernels for 60%

profile of v2, /device:TPU:0, one launch (start us, length us, event | category | flops | bytes accessed | tf_op | source)
XLA Modules:
  0.0 107.7 jit_solution(2192073769483638363)
XLA Ops:
  0.0 0.0 copy-start
  0.0 0.5 collective-permute-start
  0.5 1.8 %pad_maximum_fusion = bf16[4,8,256,128]{3,2,1,0:T(8,128)(2,1)S(1)} fusion(bf16[4,8,128,128]{3,2,1,0:T(8,128)(2,1)} %param.28, bf16[4,8,128,128]{3,2,1,0:T(8,128)(2,1)} %param.27), kind=kLoop, calls=%fused_computation.2 | loop fusion | flops 4194304 | bytes 4194304 | tf_op jit(solution)/shard_map/concatenate | solution.py:355
  2.2 1.6 %copy.27 = bf16[4,8,256,128]{3,2,0,1:T(8,128)(2,1)} copy(bf16[4,8,256,128]{3,2,1,0:T(8,128)(2,1)S(1)} %pad_maximum_fusion) | data formatting | bytes 4194304 | tf_op jit(solution)/shard_map/concatenate | solution.py:355
  3.8 0.0 copy-start.7
  3.8 0.0 copy-start.3
  3.8 0.0 copy-start.1
  3.8 7.0 %all-to-all-start = ((bf16[4,8,256,128]{3,2,0,1:T(8,128)(2,1)}), bf16[4,8,256,128]{3,2,0,1:T(8,128)(2,1)S(1)}, u32[]{:S(2)}, u32[]{:S(2)}) async-start(bf16[4,8,256,128]{3,2,0,1:T(8,128)(2,1)} %copy.27), calls=%async_computation | async-start | bytes 4194304 | tf_op jit(solution)/shard_map/all_to_all | solution.py:358
  10.8 0.2 collective-permute-start.2
  11.0 0.0 copy-done.7
  11.0 0.0 copy-done.3
  11.0 0.6 gather_fusion
  11.6 0.1 reshape.47
  11.7 0.0 copy-done.1
  11.7 0.0 copy-start.8
  11.7 0.0 copy-start.4
  11.7 1.2 %gather_fusion.1 = s32[128]{0:T(128)S(1)} fusion(s32[32]{0:T(128)S(1)} %copy-done.1, s32[1024]{0:T(1024)S(1)} %pad_clamp_fusion), kind=kCustom, calls=%fused_computation.1 | custom fusion | bytes 1536 | tf_op jit(solution)/shard_map/gather | solution.py:367
  13.0 0.1 reshape.46.order
  13.0 0.0 copy-done
  13.0 0.0 copy-done.8
  13.1 0.0 copy-done.4
  13.1 0.0 copy-start.5
  13.1 2.2 %fusion.5 = bf16[16,512]{1,0:T(8,128)(2,1)S(1)} fusion(bf16[512,2048]{1,0:T(8,128)(2,1)} %x.1, bf16[2048,8]{0,1:T(8,128)(2,1)S(1)} %get-tuple-element.34, bf16[2048,8]{0,1:T(8,128)(2,1)S(1)} %get-tuple-element.33), kind=kOutput, calls=%fused_computation.13 | convolution fusion | flops 33685504 | bytes 2179072 | tf_op jit(solution)/shard_map/dot_general | solution.py:317
  15.3 0.0 collective-permute-done.other
  15.3 2.2 %fusion.4 = bf16[16,512]{1,0:T(8,128)(2,1)S(1)} fusion(bf16[512,2048]{1,0:T(8,128)(2,1)} %collective-permute-done.other, bf16[2048,8]{0,1:T(8,128)(2,1)S(1)} %get-tuple-element.34, bf16[2048,8]{0,1:T(8,128)(2,1)S(1)} %get-tuple-element.33), kind=kOutput, calls=%fused_computation.12 | convolution fusion | flops 33685504 | bytes 2179072 | tf_op jit(solution)/shard_map/dot_general | solution.py:317
  17.6 0.0 copy-done.5
  17.6 0.1 fusion.11
  17.7 0.2 fusion.2
  18.0 0.7 pad_maximum_fusion.2
  18.6 2.0 %copy.24.cols = f32[4,1024,4]{2,1,0:T(8,128)} copy(f32[4,1024,4]{1,2,0:T(4,128)S(1)} %get-tuple-element.30) | data formatting | bytes 131072 | tf_op jit(solution)/shard_map/transpose | solution.py:116
  20.6 38.9 %shard_map.154 = (bf16[1024,1024]{1,0:T(8,128)(2,1)}, bf16[8,8,256,128]{3,2,1,0:T(8,128)(2,1)}, bf16[8,8,256,128]{3,2,1,0:T(8,128)(2,1)}, f32[8,8,128,128]{3,2,1,0:T(8,128)}) custom-call(s32[1]{0:T(128)} %bitcast.half, bf16[512,2048]{1,0:T(8,128)(2,1)} %x.1, bf16[512,2048]{1,0:T(8,128)(2,1)} %collective-permute-done.other, bf16[2048,512]{1,0:T(8,128)(2,1)} %w_q.1, ...), custom_call_target="tpu_custom_call" | custom-call | flops 59592671232 | bytes 29360128 | tf_op jit(solution)/shard_map/pallas_call | solution.py:118
  59.6 0.1 slice.18
  59.6 0.6 exp.15.closing
  60.3 0.0 all-to-all-done
  60.3 6.1 %shard_map.155 = f32[8,128,128]{2,1,0:T(8,128)} custom-call(s32[8,16]{1,0:T(8,128)S(1)} %reshape.46.order, f32[128,128]{1,0:T(8,128)S(1)} %dynamic-slice_bitcast_fusion.init, bf16[32,256,128]{2,1,0:T(8,128)(2,1)S(1)} %bitcast.30), custom_call_target="tpu_custom_call" | custom-call | flops 8589934592 | bytes 4194304 | tf_op jit(solution)/shard_map/pallas_call | solution.py:232
  66.4 5.9 %all-to-all-start.1 = ((f32[8,128,128]{2,1,0:T(8,128)}), f32[8,128,128]{2,1,0:T(8,128)S(1)}, u32[]{:S(2)}, u32[]{:S(2)}) async-start(f32[8,128,128]{2,1,0:T(8,128)} %shard_map.155), calls=%async_computation.1 | async-start | bytes 1048576 | tf_op jit(solution)/shard_map/all_to_all | solution.py:373
  72.2 11.1 %shard_map.156 = (f32[1024,1024]{1,0:T(8,128)}, bf16[1024,1024]{1,0:T(8,128)(2,1)}) custom-call(f32[8,8]{1,0:T(8,128)} %exp.15.closing, bf16[8,8,256,128]{3,2,1,0:T(8,128)(2,1)} %get-tuple-element.22.qw, bf16[8,8,256,128]{3,2,1,0:T(8,128)(2,1)} %get-tuple-element.23.at_in, f32[8,8,128,128]{3,2,1,0:T(8,128)} %get-tuple-element.24.u_in), custom_call_target="tpu_custom_call" | custom-call | flops 4294967296 | bytes 18874368 | tf_op jit(solution)/shard_map/pallas_call | solution.py:185
  83.3 4.0 %all-to-all-done.1.start = f32[8,128,128]{2,1,0:T(8,128)S(1)} async-done(((f32[8,128,128]{2,1,0:T(8,128)}), f32[8,128,128]{2,1,0:T(8,128)S(1)}, u32[]{:S(2)}, u32[]{:S(2)}) %all-to-all-start.1) | async-done | bytes 524320 | tf_op jit(solution)/shard_map/all_to_all | solution.py:373
  87.3 0.0 copy-start.2
  87.3 0.8 copy-done.2
  88.1 4.1 %shard_map.158 = bf16[512,1024]{1,0:T(8,128)(2,1)} custom-call(s32[1]{0:T(128)S(6)} %sub.5.half, f32[1024,1024]{1,0:T(8,128)} %get-tuple-element.25.core, bf16[1024,1024]{1,0:T(8,128)(2,1)} %get-tuple-element.26.linear, bf16[1024,1024]{1,0:T(8,128)(2,1)} %get-tuple-element.27.gate, f32[8,128,128]{2,1,0:T(8,128)} %copy-done.2, f32[1,128]{1,0:T(1,128)} %bitcast.33), custom_call_target="tpu_custom_call" | custom-call | flops 1073741824 | bytes 5242880 | tf_op jit(solution)/shard_map/pallas_call | solution.py:266
  92.2 0.0 collective-permute-start.1
  92.2 4.1 %shard_map.157.own = bf16[512,1024]{1,0:T(8,128)(2,1)} custom-call(s32[1]{0:T(128)} %bitcast.half, f32[1024,1024]{1,0:T(8,128)} %get-tuple-element.25.core, bf16[1024,1024]{1,0:T(8,128)(2,1)} %get-tuple-element.26.linear, bf16[1024,1024]{1,0:T(8,128)(2,1)} %get-tuple-element.27.gate, f32[8,128,128]{2,1,0:T(8,128)} %copy-done.2, f32[1,128]{1,0:T(1,128)} %bitcast.34), custom_call_target="tpu_custom_call" | custom-call | flops 1073741824 | bytes 5242880 | tf_op jit(solution)/shard_map/pallas_call | solution.py:266
  96.4 0.0 collective-permute-done.2.w_other
  96.4 0.0 collective-permute-done.1.received
  96.4 0.0 copy-start.6
  96.4 1.0 copy-done.6
  97.3 10.4 %shard_map.159 = bf16[512,2048]{1,0:T(8,128)(2,1)} custom-call(bf16[512,1024]{1,0:T(8,128)(2,1)} %shard_map.157.own, bf16[512,1024]{1,0:T(8,128)(2,1)} %copy-done.6, bf16[1024,2048]{1,0:T(8,128)(2,1)} %w_own.1, bf16[1024,2048]{1,0:T(8,128)(2,1)} %collective-permute-done.2.w_other), custom_call_target="tpu_custom_call" | custom-call | flops 4294967296 | bytes 12582912 | tf_op jit(solution)/shard_map/pallas_call | solution.py:298
  (11 shorter events, 0.1 us)
Async XLA Ops:
  0.0 13.0 %copy-start = (f32[8,128,128]{2,1,0:T(8,128)S(1)}, f32[8,128,128]{2,1,0:T(8,128)}, u32[]{:S(2)}) copy-start(f32[8,128,128]{2,1,0:T(8,128)} %param.26) | copy-start | bytes 1572868
  0.0 15.3 %collective-permute-start = (bf16[512,2048]{1,0:T(8,128)(2,1)}, bf16[512,2048]{1,0:T(8,128)(2,1)}, u32[]{:S(2)}, u32[]{:S(2)}) collective-permute-start(bf16[512,2048]{1,0:T(8,128)(2,1)} %x.1), channel_id=1, source_target_pairs={{0,1},{1,0},{2,3},{3,2},{4,5},{5,4},{6,7},{7,6},{8,9},{9,8},{10,11... | collective-permute-start | bytes 6291464 | tf_op jit(solution)/shard_map/ppermute | solution.py:359
  3.8 7.2 %copy-start.7 = (s32[8]{0:T(128)S(1)}, s32[8]{0:T(128)}, u32[]{:S(2)}) copy-start(s32[8]{0:T(128)} %param.31) | copy-start | bytes 100
  3.8 7.2 %copy-start.3 = (s32[8,16]{1,0:T(8,128)S(1)}, s32[8,16]{1,0:T(8,128)}, u32[]{:S(2)}) copy-start(s32[8,16]{1,0:T(8,128)} %param.29) | copy-start | bytes 1540
  3.8 7.9 %copy-start.1 = (s32[32]{0:T(128)S(1)}, s32[32]{0:T(128)}, u32[]{:S(2)}) copy-start(s32[32]{0:T(128)} %param.30) | copy-start | bytes 388
  3.8 56.4 %all-to-all-start = ((bf16[4,8,256,128]{3,2,0,1:T(8,128)(2,1)}), bf16[4,8,256,128]{3,2,0,1:T(8,128)(2,1)S(1)}, u32[]{:S(2)}, u32[]{:S(2)}) async-start(bf16[4,8,256,128]{3,2,0,1:T(8,128)(2,1)} %copy.27), calls=%async_computation | async-start | bytes 4194304 | tf_op jit(solution)/shard_map/all_to_all | solution.py:358
  10.8 85.5 %collective-permute-start.2 = (bf16[1024,2048]{1,0:T(8,128)(2,1)}, bf16[1024,2048]{1,0:T(8,128)(2,1)}, u32[]{:S(2)}, u32[]{:S(2)}) collective-permute-start(bf16[1024,2048]{1,0:T(8,128)(2,1)} %w_own.1), channel_id=1, source_target_pairs={{0,1},{1,0},{2,3},{3,2},{4,5},{5,4},{6,7},{7,6},{8,9},{9,8},{10,11... | collective-permute-start | bytes 12582920 | tf_op jit(solution)/shard_map/ppermute | solution.py:360
  11.7 1.4 %copy-start.8 = (f32[8]{0:T(128)S(1)}, f32[8]{0:T(128)}, u32[]{:S(2)}) copy-start(f32[8]{0:T(128)} %param.23) | copy-start | bytes 100
  11.7 1.4 %copy-start.4 = (bf16[2,2048,8]{1,2,0:T(8,128)(2,1)S(1)}, bf16[2,2048,8]{1,2,0:T(8,128)(2,1)}, u32[]{:S(2)}) copy-start(bf16[2,2048,8]{1,2,0:T(8,128)(2,1)} %param.21) | copy-start | bytes 196612
  13.1 4.5 %copy-start.5 = (f32[8]{0:T(128)S(1)}, f32[8]{0:T(128)}, u32[]{:S(2)}) copy-start(f32[8]{0:T(128)} %param.24) | copy-start | bytes 100
  66.4 21.0 %all-to-all-start.1 = ((f32[8,128,128]{2,1,0:T(8,128)}), f32[8,128,128]{2,1,0:T(8,128)S(1)}, u32[]{:S(2)}, u32[]{:S(2)}) async-start(f32[8,128,128]{2,1,0:T(8,128)} %shard_map.155), calls=%async_computation.1 | async-start | bytes 1048576 | tf_op jit(solution)/shard_map/all_to_all | solution.py:373
  87.3 0.8 copy-start.2
  92.2 4.1 %collective-permute-start.1 = (bf16[512,1024]{1,0:T(8,128)(2,1)}, bf16[512,1024]{1,0:T(8,128)(2,1)S(1)}, u32[]{:S(2)}, u32[]{:S(2)}) collective-permute-start(bf16[512,1024]{1,0:T(8,128)(2,1)} %shard_map.158), channel_id=1, source_target_pairs={{0,1},{1,0},{2,3},{3,2},{4,5},{5,4},{6,7},{7,6},{8,9},{9,8},{10,11... | collective-permute-start | bytes 3145736 | tf_op jit(solution)/shard_map/ppermute | solution.py:377
  96.4 1.0 copy-start.6

commit v3 on v2

--- a/solution.py
+++ b/solution.py
@@ -9,6 +9,8 @@
 DV = 128
 CHUNK = 128
 ROWS = 256
+GATE_ROWS = 256
+OUT_COLUMNS = 512
 BF = jnp.bfloat16
 F32 = jnp.float32
 
@@ -249,11 +251,7 @@
     del half
     for head in range(start.shape[0]):
         at = slice(head * DV, (head + 1) * DV)
-        state = start[head]
-        high = state.astype(BF)
-        low = (state - high.astype(F32)).astype(BF)
-        moved = mm(linear[:, at], jnp.concatenate([high, low], axis=1))
-        values = core[:, at] + moved[:, :DV] + moved[:, DV:]
+        values = core[:, at] + mm(linear[:, at], start[head])
         z = gate[:, at].astype(F32)
         mean = jnp.mean(values * values, axis=-1, keepdims=True)
         out[:, at] = (values * lax.rsqrt(mean + 1e-06) * gain[...] * (z * jax.nn.sigmoid(z))).astype(BF)
@@ -261,8 +259,8 @@
 
 def gated(half, core, linear, gate, start, gain):
     tokens, width = core.shape
-    tiles = tokens // 2 // ROWS
-    block = pl.BlockSpec((ROWS, width), lambda i, half: (half[0] * tiles + i, 0))
+    tiles = tokens // 2 // GATE_ROWS
+    block = pl.BlockSpec((GATE_ROWS, width), lambda i, half: (half[0] * tiles + i, 0))
     return pl.pallas_call(
         gate_kernel,
         grid_spec=pltpu.PrefetchScalarGridSpec(
@@ -275,7 +273,7 @@
                 pl.BlockSpec(start.shape, lambda i, half: (0, 0, 0)),
                 pl.BlockSpec((1, DV), lambda i, half: (0, 0)),
             ],
-            out_specs=pl.BlockSpec((ROWS, width), lambda i, half: (i, 0)),
+            out_specs=pl.BlockSpec((GATE_ROWS, width), lambda i, half: (i, 0)),
         ),
         out_shape=jax.ShapeDtypeStruct((tokens // 2, width), BF),
         compiler_params=pltpu.CompilerParams(
@@ -292,7 +290,7 @@
 def project_out(own, received, w_own, w_other):
     tokens, depth = own.shape
     width = w_own.shape[1]
-    tile = 256
+    tile = OUT_COLUMNS
     left = pl.BlockSpec((tokens, depth), lambda i: (0, 0))
     right = pl.BlockSpec((depth, tile), lambda i: (0, i))
     return pl.pallas_call(
@@ -370,7 +368,7 @@
     init, order, closing, u = lax.optimization_barrier((init, order, closing, u))
     states = compose(order, init, docs)
     states, closing = lax.optimization_barrier((states, closing))
-    start = lax.all_to_all(states, "store", split_axis=0, concat_axis=0, tiled=True)[::copies]
+    start = lax.all_to_all(states.astype(BF), "store", split_axis=0, concat_axis=0, tiled=True)[::copies]
     core, linear = scan_chunks(closing, qw, attend, u)
     gain = norm_gain.reshape(1, DV)
     away = gated(1 - half, core, linear, gate, start, gain)

time: 108 us -> 102 us (0.944)
  waiting for transfers between devices: 4.06 us -> 0.01 us
  Pallas kernels: 74.7 us -> 71.7 us
    all_to_all x1, waiting for transfers between devices: 4.05 us -> 0.01 us  [on_device(): lax.all_to_all(states.astype(BF), 'store', split_axis=0, concat_axis=0, t...]
    pallas_call x1, Pallas kernels: 10.4 us -> 8.63 us  [project_out(): pl.pallas_call(project_kernel, grid=(width // tile,), in_specs=[left, lef...]
  transfers between devices with their start and end apart: 5 -> 5, of which waited for: 1 -> 0; matrix products, arithmetic and copies ran while one was open for 13% -> 14% of each run, Pallas kernels for 60% -> 62%
where the time goes in v3:
time: 102 us
  Pallas kernels  71.7 us (70%)
  starting transfers between devices  13.7 us (13%)
  local copies, waits for them, and re-layouts  7.94 us (8%)
  matrix products  4.66 us (5%)
  other arithmetic  3.34 us (3%)
    pallas_call x1, Pallas kernels, chunk_terms(): pl.pallas_call(terms_kernel, grid=(steps,), in_specs=[pl.BlockSpec(memory...  38.9 us
    pallas_call x1, Pallas kernels, scan_chunks(): pl.pallas_call(scan_kernel, grid=(chunks,), in_specs=[pl.BlockSpec(memory...  11.1 us
    pallas_call x1, Pallas kernels, project_out(): pl.pallas_call(project_kernel, grid=(width // tile,), in_specs=[left, lef...  8.63 us
    pallas_call x2, Pallas kernels, gated(): pl.pallas_call(gate_kernel, grid_spec=pltpu.PrefetchScalarGridSpec(num_sc...  7.74 us
    all_to_all x1, starting transfers between devices, on_device(): lax.all_to_all(docs, 'store', split_axis=1, concat_axis=0, tiled=True)[:, 0]  7.03 us
    all_to_all x1, starting transfers between devices, on_device(): lax.all_to_all(states.astype(BF), 'store', split_axis=0, concat_axis=0, t...  5.85 us
    pallas_call x1, Pallas kernels, compose(): pl.pallas_call(compose_kernel, in_specs=[pl.BlockSpec(memory_space=pltpu....  5.29 us
    dot_general x2, matrix products, decays(): lax.dot_general(weights, part, (((0,), (1,)), ((), ())), preferred_elemen...  4.49 us
  transfers between devices with their start and end apart: 5, of which 0 were waited for; matrix products, arithmetic and copies ran while one was open for 14% of the time, Pallas kernels for 62%

profile of v3, /device:TPU:0, one launch (start us, length us, event | category | flops | bytes accessed | tf_op | source)
XLA Modules:
  0.0 101.5 jit_solution(7805272032317094065)
XLA Ops:
  0.0 0.0 copy-start
  0.0 0.5 collective-permute-start
  0.5 1.8 %pad_maximum_fusion = bf16[4,8,256,128]{3,2,1,0:T(8,128)(2,1)S(1)} fusion(bf16[4,8,128,128]{3,2,1,0:T(8,128)(2,1)} %param.28, bf16[4,8,128,128]{3,2,1,0:T(8,128)(2,1)} %param.27), kind=kLoop, calls=%fused_computation.2 | loop fusion | flops 4194304 | bytes 4194304 | tf_op jit(solution)/shard_map/concatenate | solution.py:353
  2.2 1.6 %copy.27 = bf16[4,8,256,128]{3,2,0,1:T(8,128)(2,1)} copy(bf16[4,8,256,128]{3,2,1,0:T(8,128)(2,1)S(1)} %pad_maximum_fusion) | data formatting | bytes 4194304 | tf_op jit(solution)/shard_map/concatenate | solution.py:353
  3.8 0.0 copy-start.7
  3.8 0.0 copy-start.3
  3.8 0.0 copy-start.1
  3.8 7.0 %all-to-all-start = ((bf16[4,8,256,128]{3,2,0,1:T(8,128)(2,1)}), bf16[4,8,256,128]{3,2,0,1:T(8,128)(2,1)S(1)}, u32[]{:S(2)}, u32[]{:S(2)}) async-start(bf16[4,8,256,128]{3,2,0,1:T(8,128)(2,1)} %copy.27), calls=%async_computation | async-start | bytes 4194304 | tf_op jit(solution)/shard_map/all_to_all | solution.py:356
  10.8 0.2 collective-permute-start.2
  11.0 0.0 copy-done.7
  11.0 0.0 copy-done.3
  11.0 0.6 gather_fusion
  11.6 0.1 reshape.47
  11.7 0.0 copy-done.1
  11.7 0.0 copy-start.8
  11.7 0.0 copy-start.4
  11.7 1.2 %gather_fusion.1 = s32[128]{0:T(128)S(1)} fusion(s32[32]{0:T(128)S(1)} %copy-done.1, s32[1024]{0:T(1024)S(1)} %pad_clamp_fusion), kind=kCustom, calls=%fused_computation.1 | custom fusion | bytes 1536 | tf_op jit(solution)/shard_map/gather | solution.py:365
  13.0 0.1 reshape.46.order
  13.0 0.0 copy-done
  13.0 0.0 copy-done.8
  13.1 0.0 copy-done.4
  13.1 0.0 copy-start.5
  13.1 2.2 %fusion.5 = bf16[16,512]{1,0:T(8,128)(2,1)S(1)} fusion(bf16[512,2048]{1,0:T(8,128)(2,1)} %x.1, bf16[2048,8]{0,1:T(8,128)(2,1)S(1)} %get-tuple-element.34, bf16[2048,8]{0,1:T(8,128)(2,1)S(1)} %get-tuple-element.33), kind=kOutput, calls=%fused_computation.13 | convolution fusion | flops 33685504 | bytes 2179072 | tf_op jit(solution)/shard_map/dot_general | solution.py:315
  15.3 0.0 collective-permute-done.other
  15.3 2.2 %fusion.4 = bf16[16,512]{1,0:T(8,128)(2,1)S(1)} fusion(bf16[512,2048]{1,0:T(8,128)(2,1)} %collective-permute-done.other, bf16[2048,8]{0,1:T(8,128)(2,1)S(1)} %get-tuple-element.34, bf16[2048,8]{0,1:T(8,128)(2,1)S(1)} %get-tuple-element.33), kind=kOutput, calls=%fused_computation.12 | convolution fusion | flops 33685504 | bytes 2179072 | tf_op jit(solution)/shard_map/dot_general | solution.py:315
  17.6 0.0 copy-done.5
  17.6 0.1 fusion.11
  17.7 0.2 fusion.2
  18.0 0.7 pad_maximum_fusion.2
  18.6 2.0 %copy.24.cols = f32[4,1024,4]{2,1,0:T(8,128)} copy(f32[4,1024,4]{1,2,0:T(4,128)S(1)} %get-tuple-element.30) | data formatting | bytes 131072 | tf_op jit(solution)/shard_map/transpose | solution.py:118
  20.6 38.9 %shard_map.154 = (bf16[1024,1024]{1,0:T(8,128)(2,1)}, bf16[8,8,256,128]{3,2,1,0:T(8,128)(2,1)}, bf16[8,8,256,128]{3,2,1,0:T(8,128)(2,1)}, f32[8,8,128,128]{3,2,1,0:T(8,128)}) custom-call(s32[1]{0:T(128)} %bitcast.half, bf16[512,2048]{1,0:T(8,128)(2,1)} %x.1, bf16[512,2048]{1,0:T(8,128)(2,1)} %collective-permute-done.other, bf16[2048,512]{1,0:T(8,128)(2,1)} %w_q.1, ...), custom_call_target="tpu_custom_call" | custom-call | flops 59592671232 | bytes 29360128 | tf_op jit(solution)/shard_map/pallas_call | solution.py:120
  59.6 0.1 slice.18
  59.6 0.6 exp.15.closing
  60.3 0.0 all-to-all-done
  60.3 5.3 %shard_map.155 = f32[8,128,128]{2,1,0:T(8,128)S(1)} custom-call(s32[8,16]{1,0:T(8,128)S(1)} %reshape.46.order, f32[128,128]{1,0:T(8,128)S(1)} %dynamic-slice_bitcast_fusion.init, bf16[32,256,128]{2,1,0:T(8,128)(2,1)S(1)} %bitcast.30), custom_call_target="tpu_custom_call" | custom-call | flops 8589934592 | bytes 4194304 | tf_op jit(solution)/shard_map/pallas_call | solution.py:234
  65.6 0.8 convert_element_type.12
  66.3 5.9 %all-to-all-start.1 = ((bf16[8,128,128]{2,1,0:T(8,128)(2,1)}), bf16[8,128,128]{2,1,0:T(8,128)(2,1)S(1)}, u32[]{:S(2)}, u32[]{:S(2)}) async-start(bf16[8,128,128]{2,1,0:T(8,128)(2,1)} %convert_element_type.12), calls=%async_computation.1 | async-start | bytes 524288 | tf_op jit(solution)/shard_map/all_to_all | solution.py:371
  72.2 11.1 %shard_map.156 = (f32[1024,1024]{1,0:T(8,128)}, bf16[1024,1024]{1,0:T(8,128)(2,1)}) custom-call(f32[8,8]{1,0:T(8,128)} %exp.15.closing, bf16[8,8,256,128]{3,2,1,0:T(8,128)(2,1)} %get-tuple-element.22.qw, bf16[8,8,256,128]{3,2,1,0:T(8,128)(2,1)} %get-tuple-element.23.at_in, f32[8,8,128,128]{3,2,1,0:T(8,128)} %get-tuple-element.24.u_in), custom_call_target="tpu_custom_call" | custom-call | flops 4294967296 | bytes 18874368 | tf_op jit(solution)/shard_map/pallas_call | solution.py:187
  83.3 0.0 all-to-all-done.1.start
  83.3 0.0 copy-start.2
  83.3 0.7 copy-done.2
  84.0 3.9 %shard_map.158 = bf16[512,1024]{1,0:T(8,128)(2,1)} custom-call(s32[1]{0:T(128)S(6)} %sub.5.half, f32[1024,1024]{1,0:T(8,128)} %get-tuple-element.25.core, bf16[1024,1024]{1,0:T(8,128)(2,1)} %get-tuple-element.26.linear, bf16[1024,1024]{1,0:T(8,128)(2,1)} %get-tuple-element.27.gate, bf16[8,128,128]{2,1,0:T(8,128)(2,1)} %copy-done.2, f32[1,128]{1,0:T(1,128)} %bitcast.33), custom_call_target="tpu_custom_call" | custom-call | flops 1073741824 | bytes 5242880 | tf_op jit(solution)/shard_map/pallas_call | solution.py:264
  87.8 0.2 collective-permute-start.1
  88.0 3.9 %shard_map.157.own = bf16[512,1024]{1,0:T(8,128)(2,1)} custom-call(s32[1]{0:T(128)} %bitcast.half, f32[1024,1024]{1,0:T(8,128)} %get-tuple-element.25.core, bf16[1024,1024]{1,0:T(8,128)(2,1)} %get-tuple-element.26.linear, bf16[1024,1024]{1,0:T(8,128)(2,1)} %get-tuple-element.27.gate, bf16[8,128,128]{2,1,0:T(8,128)(2,1)} %copy-done.2, f32[1,128]{1,0:T(1,128)} %bitcast.34), custom_call_target="tpu_custom_call" | custom-call | flops 1073741824 | bytes 5242880 | tf_op jit(solution)/shard_map/pallas_call | solution.py:264
  91.9 0.0 collective-permute-done.2.w_other
  91.9 0.0 collective-permute-done.1.received
  91.9 0.0 copy-start.6
  91.9 1.0 copy-done.6
  92.9 8.6 %shard_map.159 = bf16[512,2048]{1,0:T(8,128)(2,1)} custom-call(bf16[512,1024]{1,0:T(8,128)(2,1)} %shard_map.157.own, bf16[512,1024]{1,0:T(8,128)(2,1)} %copy-done.6, bf16[1024,2048]{1,0:T(8,128)(2,1)} %w_own.1, bf16[1024,2048]{1,0:T(8,128)(2,1)} %collective-permute-done.2.w_other), custom_call_target="tpu_custom_call" | custom-call | flops 4294967296 | bytes 12582912 | tf_op jit(solution)/shard_map/pallas_call | solution.py:296
  (11 shorter events, 0.1 us)
Async XLA Ops:
  0.0 13.0 %copy-start = (f32[8,128,128]{2,1,0:T(8,128)S(1)}, f32[8,128,128]{2,1,0:T(8,128)}, u32[]{:S(2)}) copy-start(f32[8,128,128]{2,1,0:T(8,128)} %param.26) | copy-start | bytes 1572868
  0.0 15.3 %collective-permute-start = (bf16[512,2048]{1,0:T(8,128)(2,1)}, bf16[512,2048]{1,0:T(8,128)(2,1)}, u32[]{:S(2)}, u32[]{:S(2)}) collective-permute-start(bf16[512,2048]{1,0:T(8,128)(2,1)} %x.1), channel_id=1, source_target_pairs={{0,1},{1,0},{2,3},{3,2},{4,5},{5,4},{6,7},{7,6},{8,9},{9,8},{10,11... | collective-permute-start | bytes 6291464 | tf_op jit(solution)/shard_map/ppermute | solution.py:357
  3.8 7.2 %copy-start.7 = (s32[8]{0:T(128)S(1)}, s32[8]{0:T(128)}, u32[]{:S(2)}) copy-start(s32[8]{0:T(128)} %param.31) | copy-start | bytes 100
  3.8 7.2 %copy-start.3 = (s32[8,16]{1,0:T(8,128)S(1)}, s32[8,16]{1,0:T(8,128)}, u32[]{:S(2)}) copy-start(s32[8,16]{1,0:T(8,128)} %param.29) | copy-start | bytes 1540
  3.8 7.9 %copy-start.1 = (s32[32]{0:T(128)S(1)}, s32[32]{0:T(128)}, u32[]{:S(2)}) copy-start(s32[32]{0:T(128)} %param.30) | copy-start | bytes 388
  3.8 56.4 %all-to-all-start = ((bf16[4,8,256,128]{3,2,0,1:T(8,128)(2,1)}), bf16[4,8,256,128]{3,2,0,1:T(8,128)(2,1)S(1)}, u32[]{:S(2)}, u32[]{:S(2)}) async-start(bf16[4,8,256,128]{3,2,0,1:T(8,128)(2,1)} %copy.27), calls=%async_computation | async-start | bytes 4194304 | tf_op jit(solution)/shard_map/all_to_all | solution.py:356
  10.8 81.1 %collective-permute-start.2 = (bf16[1024,2048]{1,0:T(8,128)(2,1)}, bf16[1024,2048]{1,0:T(8,128)(2,1)}, u32[]{:S(2)}, u32[]{:S(2)}) collective-permute-start(bf16[1024,2048]{1,0:T(8,128)(2,1)} %w_own.1), channel_id=1, source_target_pairs={{0,1},{1,0},{2,3},{3,2},{4,5},{5,4},{6,7},{7,6},{8,9},{9,8},{10,11... | collective-permute-start | bytes 12582920 | tf_op jit(solution)/shard_map/ppermute | solution.py:358
  11.7 1.4 %copy-start.8 = (f32[8]{0:T(128)S(1)}, f32[8]{0:T(128)}, u32[]{:S(2)}) copy-start(f32[8]{0:T(128)} %param.23) | copy-start | bytes 100
  11.7 1.4 %copy-start.4 = (bf16[2,2048,8]{1,2,0:T(8,128)(2,1)S(1)}, bf16[2,2048,8]{1,2,0:T(8,128)(2,1)}, u32[]{:S(2)}) copy-start(bf16[2,2048,8]{1,2,0:T(8,128)(2,1)} %param.21) | copy-start | bytes 196612
  13.1 4.5 %copy-start.5 = (f32[8]{0:T(128)S(1)}, f32[8]{0:T(128)}, u32[]{:S(2)}) copy-start(f32[8]{0:T(128)} %param.24) | copy-start | bytes 100
  66.3 16.9 %all-to-all-start.1 = ((bf16[8,128,128]{2,1,0:T(8,128)(2,1)}), bf16[8,128,128]{2,1,0:T(8,128)(2,1)S(1)}, u32[]{:S(2)}, u32[]{:S(2)}) async-start(bf16[8,128,128]{2,1,0:T(8,128)(2,1)} %convert_element_type.12), calls=%async_computation.1 | async-start | bytes 524288 | tf_op jit(solution)/shard_map/all_to_all | solution.py:371
  83.3 0.7 copy-start.2
  87.8 4.1 %collective-permute-start.1 = (bf16[512,1024]{1,0:T(8,128)(2,1)}, bf16[512,1024]{1,0:T(8,128)(2,1)S(1)}, u32[]{:S(2)}, u32[]{:S(2)}) collective-permute-start(bf16[512,1024]{1,0:T(8,128)(2,1)} %shard_map.158), channel_id=1, source_target_pairs={{0,1},{1,0},{2,3},{3,2},{4,5},{5,4},{6,7},{7,6},{8,9},{9,8},{10,11... | collective-permute-start | bytes 3145736 | tf_op jit(solution)/shard_map/ppermute | solution.py:375
  91.9 1.0 copy-start.6
